TPU v7x, 128 devices: a whole 4x4x4 slice. The times are simulated.
128 devices in a mesh: owner: 32 (over x, y, core), dp: 4 (over z).
Axes of the slice: x: 4, y: 4, z: 4, core: 2. Of those that a mesh axis runs over, the one named last changes fastest.
Arguments:
- entity_table: float32 [65536, 400], P('owner'), may hold values from -0.2 to 0.2
- entity_state: float32 [65536], P('owner'), may hold values from 0.002 to 0.02
- phase_table: float32 [7424, 200], replicated, may hold values from -3.1416 to 3.1416
- phase_state: float32 [7424], replicated, may hold values from 1e-05 to 0.0001
- pull_rows: int32 [128, 32, 128], P(('owner', 'dp')), may hold values from 0 to 2047
- head_slot: int32 [128, 512], P(('owner', 'dp')), may hold values from 0 to 4095, as said below
- tail_slot: int32 [128, 512], P(('owner', 'dp')), may hold values from 0 to 4095, as said below
- neg_slot: int32 [128, 2, 1024], P(('owner', 'dp')), may hold values from 0 to 4095, as said below
- relation: int32 [128, 512], P(('owner', 'dp')), may hold values from 0 to 7423
Outputs:
- new_entity: float32 [65536, 400], P('owner')
- new_entity_state: float32 [65536], P('owner')
- new_phase: float32 [7424, 200], replicated
- new_phase_state: float32 [7424], replicated
Inputs may be any that keep to these rules, and one draw needn't show every extreme that they name: `head_slot`: slot numbers of the worker's pulled rows, owner-major. `tail_slot`: slot numbers of the worker's pulled rows, owner-major. `neg_slot`: slot numbers of the worker's pulled rows, owner-major.
All inputs are finite; a program needn't handle non-finite values.
Results may differ from a plain program's by a relative error of at most 0.0035.
Values may be sent and summed in bfloat16 or wider, within the bound.
A program may use at most 192 MiB of HBM per device.

v0:
```python
import jax
import jax.numpy as jnp
from jax import lax
from jax.sharding import PartitionSpec as P

GROUP = 256
GROUPS = 2


GAMMA = 2.0
RATE = 0.05


def block_grads(heads, tails, negs, phase):
    width = phase.shape[1]
    cosine = jnp.cos(phase)
    sine = jnp.sin(phase)
    head_re = heads[:, :width].astype(jnp.float32)
    head_im = heads[:, width:].astype(jnp.float32)
    rot_re = head_re * cosine - head_im * sine
    rot_im = head_re * sine + head_im * cosine
    rotated = jnp.concatenate([rot_re, rot_im], 1)
    diff = rotated - tails.astype(jnp.float32)
    pos_score = GAMMA - jnp.sum(diff * diff, 1)
    rot_half = rotated.astype(jnp.bfloat16)
    rot_wide = rot_half.astype(jnp.float32)
    neg_wide = negs.astype(jnp.float32)
    row_norm = jnp.sum(rot_wide * rot_wide, 1)
    neg_norm = jnp.sum(neg_wide * neg_wide, 1)
    cross = lax.dot_general(
        rot_half, negs, (((1,), (1,)), ((), ())), preferred_element_type=jnp.float32
    )
    neg_score = GAMMA - (row_norm[:, None] + neg_norm[None, :] - 2.0 * cross)
    diff_grad = 2.0 * jax.nn.sigmoid(-pos_score)[:, None] * diff
    neg_weight = jax.nn.sigmoid(neg_score) / negs.shape[0]
    weight_half = neg_weight.astype(jnp.bfloat16)
    rot_grad = (
        diff_grad
        - 2.0 * jnp.sum(neg_weight, 1)[:, None] * rot_wide
        + 2.0 * jnp.dot(weight_half, negs, preferred_element_type=jnp.float32)
    )
    neg_grad = -2.0 * jnp.sum(neg_weight, 0)[:, None] * neg_wide + 2.0 * lax.dot_general(
        weight_half, rot_half, (((0,), (0,)), ((), ())), preferred_element_type=jnp.float32
    )
    grad_re = rot_grad[:, :width]
    grad_im = rot_grad[:, width:]
    phase_grad = grad_im * rot_re - grad_re * rot_im
    head_grad = jnp.concatenate(
        [grad_re * cosine + grad_im * sine, grad_im * cosine - grad_re * sine], 1
    )
    return (head_grad, -diff_grad, neg_grad, phase_grad)


def adagrad(table, state, grad):
    new_state = state + jnp.mean(grad * grad, 1)
    return (table - RATE * grad / jnp.sqrt(new_state)[:, None], new_state)


def on_device(
    entity_table,
    entity_state,
    phase_table,
    phase_state,
    pull_rows,
    head_slot,
    tail_slot,
    neg_slot,
    relation,
):
    owners = lax.axis_size("owner")
    width_two = entity_table.shape[1]
    requests = pull_rows[0]
    capacity = requests.shape[1]
    asked = lax.all_to_all(requests, "owner", split_axis=0, concat_axis=0, tiled=True)
    fetched = jnp.take(entity_table, asked.reshape(-1), axis=0).astype(jnp.bfloat16)
    fetched = fetched.reshape(asked.shape + (width_two,))
    returned_rows = lax.all_to_all(fetched, "owner", split_axis=0, concat_axis=0, tiled=True)
    pulled = returned_rows
    pulled = pulled.reshape(owners * capacity, width_two)
    slot_grad = jnp.zeros((owners * capacity, width_two), jnp.float32)
    rel_grad = jnp.zeros(phase_table.shape, jnp.float32)
    for block in range(GROUPS):
        hs = head_slot[0, block * GROUP : (block + 1) * GROUP]
        ts = tail_slot[0, block * GROUP : (block + 1) * GROUP]
        ns = neg_slot[0, block]
        rs = relation[0, block * GROUP : (block + 1) * GROUP]
        heads = jnp.take(pulled, hs, axis=0)
        tails = jnp.take(pulled, ts, axis=0)
        negs = jnp.take(pulled, ns, axis=0)
        phase = jnp.take(phase_table, rs, axis=0)
        hg, tg, ng, pg = block_grads(heads, tails, negs, phase)
        slot_grad = slot_grad.at[hs].add(hg).at[ts].add(tg).at[ns].add(ng)
        rel_grad = rel_grad.at[rs].add(pg)
    received = lax.all_to_all(
        slot_grad.reshape(owners, capacity, width_two).astype(jnp.bfloat16),
        "owner",
        split_axis=0,
        concat_axis=0,
        tiled=True,
    ).astype(jnp.float32)
    empty = jnp.zeros(entity_table.shape, jnp.float32)
    local_sum = empty.at[asked.reshape(-1)].add(received.reshape(-1, width_two))
    entity_grad = lax.psum(local_sum, "dp")
    new_entity, new_entity_state = adagrad(entity_table, entity_state, entity_grad)
    rel_total = lax.psum(rel_grad, ("owner", "dp"))
    new_phase, new_phase_state = adagrad(phase_table, phase_state, rel_total)
    return (new_entity, new_entity_state, new_phase, new_phase_state)


def solution(mesh):
    placed = (
        P("owner", None),
        P("owner"),
        P(),
        P(),
        P(("owner", "dp"), None, None),
        P(("owner", "dp"), None),
        P(("owner", "dp"), None),
        P(("owner", "dp"), None, None),
        P(("owner", "dp"), None),
    )
    return jax.shard_map(
        on_device,
        mesh=mesh,
        in_specs=placed,
        out_specs=(P("owner", None), P("owner"), P(), P()),
        check_vma=False,
    )
```

profile of v0, /device:TPU:1, one launch (start us, length us, event | category | flops | bytes accessed | tf_op | source)
XLA Modules:
  0.0 553.4 jit_solution(10451071131643964850)
XLA Ops:
  7.2 8.6 %all-to-all-start = ((s32[32,1,128]{2,1,0:T(1,128)}), s32[32,1,128]{2,1,0:T(1,128)S(1)}, u32[]{:S(2)}, u32[]{:S(2)}) async-start(s32[32,1,128]{2,1,0:T(1,128)} %bitcast.67), calls=%async_computation | async-start | bytes 32768 | tf_op jit(solution)/shard_map/all_to_all | solution.py:74
  22.1 5.0 copy.95
  27.1 19.6 %gather_fusion = bf16[4096,400]{1,0:T(8,128)(2,1)} fusion(f32[2048,400]{1,0:T(8,128)} %copy.95, s32[4096]{0:T(1024)S(1)} %broadcast_clamp_fusion), kind=kCustom, calls=%fused_computation.8 | custom fusion | bytes 6569984 | tf_op jit(solution)/shard_map/jit(_take)/gather | solution.py:75
  46.7 8.3 %copy.74 = bf16[32,128,400]{1,2,0:T(8,128)(2,1)S(1)} copy(bf16[32,128,400]{2,1,0:T(8,128)(2,1)} %bitcast.55) | data formatting | bytes 6553600 | tf_op jit(solution)/shard_map/jit(_take)/gather | solution.py:75
  55.1 2.5 select_convert_fusion
  57.5 7.4 %all-to-all-start.1 = ((bf16[32,128,400]{1,2,0:T(8,128)(2,1)}), bf16[32,128,400]{1,2,0:T(8,128)(2,1)S(1)}, u32[]{:S(2)}, u32[]{:S(2)}) async-start(bf16[32,128,400]{1,2,0:T(8,128)(2,1)} %select_convert_fusion), calls=%async_computation.1 | async-start | bytes 6553600 | tf_op jit(solution)/shard_map/all_to_all | solution.py:77
  65.5 8.0 %copy.77 = f32[7424,200]{1,0:T(8,128)} copy(f32[7424,200]{0,1:T(8,128)} %param.17) | data formatting | bytes 11878400 | tf_op args[2]
  73.5 4.3 gather_fusion.6
  78.6 5.0 gather_fusion.2
  92.7 13.3 %all-to-all-done.1 = bf16[32,128,400]{1,2,0:T(8,128)(2,1)S(1)} async-done(((bf16[32,128,400]{1,2,0:T(8,128)(2,1)}), bf16[32,128,400]{1,2,0:T(8,128)(2,1)S(1)}, u32[]{:S(2)}, u32[]{:S(2)}) %all-to-all-start.1) | async-done | bytes 3276832 | tf_op jit(solution)/shard_map/all_to_all | solution.py:77
  106.0 7.4 %copy.75 = bf16[32,128,400]{2,1,0:T(8,128)(2,1)} copy(bf16[32,128,400]{1,2,0:T(8,128)(2,1)S(1)} %all-to-all-done.1) | data formatting | bytes 6553600 | tf_op jit(solution)/shard_map/all_to_all | solution.py:77
  113.4 4.1 gather_fusion.5
  117.7 4.1 gather_fusion.7
  122.9 1.6 fusion.28
  124.4 6.8 %gather_fusion.8 = bf16[1024,400]{1,0:T(8,128)(2,1)S(1)} fusion(bf16[4096,400]{1,0:T(8,128)(2,1)} %bitcast.51, s32[1024]{0:T(1024)S(1)} %fusion.45), kind=kCustom, calls=%fused_computation.7.clone | custom fusion | bytes 1642496 | tf_op jit(solution)/shard_map/jit(_take)/gather | solution.py:89
  134.1 1.6 multiply_add_fusion
  135.7 4.1 gather_fusion.1
  139.9 4.1 gather_fusion.3
  146.0 6.7 %gather_fusion.4 = bf16[1024,400]{1,0:T(8,128)(2,1)S(1)} fusion(bf16[4096,400]{1,0:T(8,128)(2,1)} %bitcast.54, s32[1024]{0:T(1024)S(1)} %fusion.44), kind=kCustom, calls=%fused_computation.2.clone | custom fusion | bytes 1642496 | tf_op jit(solution)/shard_map/jit(_take)/gather | solution.py:89
  153.5 1.8 fusion.51
  155.8 1.6 multiply_add_fusion.1
  157.5 1.6 fusion.9
  159.0 1.8 copy.91
  162.9 2.7 fusion.7
  165.6 3.0 copy.83
  172.9 6.3 %scatter_custom_fusion = f32[4096,400]{1,0:T(8,128)} fusion(s32[256]{0:T(256)} %bitcast.84, f32[256,400]{1,0:T(8,128)} %copy.81, f32[]{:T(128)} %constant.38.clone.1), kind=kCustom, calls=%fused_computation.23 | custom fusion | flops 102400 | bytes 6554112 | tf_op jit(solution)/shard_map/scatter-add | solution.py:92
  179.2 9.1 %scatter_fusion = f32[4096,400]{1,0:T(8,128)} fusion(f32[4096,400]{1,0:T(8,128)} %scatter_custom_fusion, s32[256]{0:T(256)S(1)} %bitcast.70, f32[256,400]{1,0:T(8,128)} %copy.82), kind=kCustom, calls=%fused_computation.10 | custom fusion | flops 102400 | bytes 1229824 | tf_op jit(solution)/shard_map/scatter-add | solution.py:92
  188.3 13.8 %scatter_fusion.1 = f32[4096,400]{1,0:T(8,128)} fusion(f32[4096,400]{1,0:T(8,128)} %scatter_fusion, s32[1024]{0:T(1024)S(1)} %bitcast.66, f32[1024,400]{1,0:T(8,128)} %copy.83), kind=kCustom, calls=%fused_computation.11 | custom fusion | flops 409600 | bytes 4919296 | tf_op jit(solution)/shard_map/scatter-add | solution.py:92
  202.1 8.6 %scatter_fusion.2 = f32[4096,400]{1,0:T(8,128)} fusion(f32[4096,400]{1,0:T(8,128)} %scatter_fusion.1, s32[256]{0:T(256)S(1)} %bitcast.69, f32[256,400]{1,0:T(8,128)S(1)} %copy.89), kind=kCustom, calls=%fused_computation.12 | custom fusion | flops 102400 | bytes 1229824 | tf_op jit(solution)/shard_map/scatter-add | solution.py:92
  210.8 8.6 %scatter_fusion.3 = f32[4096,400]{1,0:T(8,128)} fusion(f32[4096,400]{1,0:T(8,128)} %scatter_fusion.2, s32[256]{0:T(256)S(1)} %bitcast.68, f32[256,400]{1,0:T(8,128)S(1)} %copy.90), kind=kCustom, calls=%fused_computation.13 | custom fusion | flops 102400 | bytes 1229824 | tf_op jit(solution)/shard_map/scatter-add | solution.py:92
  219.4 13.3 %scatter_fusion.4 = f32[4096,400]{1,0:T(8,128)} fusion(f32[4096,400]{1,0:T(8,128)} %scatter_fusion.3, s32[1024]{0:T(1024)S(1)} %bitcast.65, f32[1024,400]{1,0:T(8,128)S(1)} %copy.91), kind=kCustom, calls=%fused_computation.14 | custom fusion | flops 409600 | bytes 4919296 | tf_op jit(solution)/shard_map/scatter-add | solution.py:92
  232.7 5.9 %convert_element_type.68 = bf16[4096,400]{1,0:T(8,128)(2,1)} convert(f32[4096,400]{1,0:T(8,128)} %scatter_fusion.4) | non-fusion elementwise | flops 1638400 | bytes 9830400 | tf_op jit(solution)/shard_map/convert_element_type | solution.py:95
  238.7 6.0 %copy.92 = bf16[32,128,400]{1,2,0:T(8,128)(2,1)} copy(bf16[32,128,400]{2,1,0:T(8,128)(2,1)} %bitcast.56) | data formatting | bytes 6553600 | tf_op jit(solution)/shard_map/convert_element_type | solution.py:95
  244.7 5.8 %all-to-all-start.2 = ((bf16[32,128,400]{1,2,0:T(8,128)(2,1)}), bf16[32,128,400]{1,2,0:T(8,128)(2,1)S(1)}, u32[]{:S(2)}, u32[]{:S(2)}) async-start(bf16[32,128,400]{1,2,0:T(8,128)(2,1)} %copy.92), calls=%async_computation.2 | async-start | bytes 6553600 | tf_op jit(solution)/shard_map/all_to_all | solution.py:94
  252.2 1.8 copy.96
  254.0 5.9 %scatter_custom_fusion.7 = f32[7424,200]{1,0:T(8,128)} fusion(s32[256]{0:T(256)} %bitcast.85, f32[256,200]{1,0:T(8,128)} %copy.96, f32[]{:T(128)} %constant.38.clone.1), kind=kCustom, calls=%fused_computation.25 | custom fusion | flops 51200 | bytes 5939712 | tf_op jit(solution)/shard_map/scatter-add | solution.py:93
  259.9 8.2 %scatter_fusion.5 = f32[7424,200]{1,0:T(8,128)} fusion(f32[7424,200]{1,0:T(8,128)} %scatter_custom_fusion.7, s32[256]{0:T(256)} %bitcast.71, f32[256,200]{1,0:T(8,128)S(1)} %copy.97), kind=kCustom, calls=%fused_computation.17 | custom fusion | flops 51200 | bytes 615424 | tf_op jit(solution)/shard_map/scatter-add | solution.py:93
  268.1 26.5 %all-to-all-done.2 = bf16[32,128,400]{1,2,0:T(8,128)(2,1)S(1)} async-done(((bf16[32,128,400]{1,2,0:T(8,128)(2,1)}), bf16[32,128,400]{1,2,0:T(8,128)(2,1)S(1)}, u32[]{:S(2)}, u32[]{:S(2)}) %all-to-all-start.2) | async-done | bytes 3276832 | tf_op jit(solution)/shard_map/all_to_all | solution.py:94
  294.6 8.5 %copy.101 = f32[32,128,400]{2,1,0:T(8,128)} copy(bf16[32,128,400]{1,2,0:T(8,128)(2,1)S(1)} %all-to-all-done.2) | data formatting | bytes 9830400 | tf_op jit(solution)/shard_map/reshape | solution.py:102
  303.1 27.6 %scatter_custom_fusion.6 = f32[2048,400]{1,0:T(8,128)} fusion(s32[4096]{0:T(1024)S(1)} %bitcast.60, f32[4096,400]{1,0:T(8,128)} %bitcast.57, f32[]{:T(128)} %constant.38.clone.1), kind=kCustom, calls=%fused_computation.27 | custom fusion | flops 1638400 | bytes 3277312 | tf_op jit(solution)/shard_map/scatter-add | solution.py:102
  330.8 108.0 %all-reduce.5.cloned.1.call-done = f32[7424,200]{1,0:T(8,128)} async-done(((f32[7424,200]{1,0:T(8,128)}), f32[7424,200]{1,0:T(8,128)}) %all-reduce.5.cloned.1.call-update) | async-done | bytes 5939216 | tf_op jit(solution)/shard_map/psum | solution.py:105
  438.8 4.4 multiply_reduce_fusion
  444.1 7.1 %divide_subtract_fusion = f32[7424,200]{1,0:T(8,128)} fusion(f32[7424,200]{1,0:T(8,128)} %copy.77, f32[7424,200]{1,0:T(8,128)S(1)} %copy-done.1, f32[7424]{0:T(1024)S(1)} %get-tuple-element.23), kind=kLoop, calls=%fused_computation.18 | loop fusion | flops 4454400 | bytes 17847296 | tf_op jit(solution)/shard_map/sub | solution.py:56
  451.1 8.3 %copy.100 = f32[7424,200]{0,1:T(8,128)} copy(f32[7424,200]{1,0:T(8,128)} %divide_subtract_fusion) | data formatting | bytes 11878400
  459.4 73.2 %all-reduce.3.cloned.1.call-done = f32[2048,400]{1,0:T(8,128)} async-done(((f32[2048,400]{1,0:T(8,128)}), f32[2048,400]{1,0:T(8,128)}) %all-reduce.3.cloned.1.call-update) | async-done | bytes 3276816 | tf_op jit(solution)/shard_map/psum | solution.py:103
  532.6 2.7 multiply_reduce_fusion.1
  536.1 4.9 divide_subtract_fusion.1
  540.9 5.2 copy.99
  (125 shorter events, 33.9 us)
Async XLA Ops:
  7.2 19.9 %all-to-all-start = ((s32[32,1,128]{2,1,0:T(1,128)}), s32[32,1,128]{2,1,0:T(1,128)S(1)}, u32[]{:S(2)}, u32[]{:S(2)}) async-start(s32[32,1,128]{2,1,0:T(1,128)} %bitcast.67), calls=%async_computation | async-start | bytes 32768 | tf_op jit(solution)/shard_map/all_to_all | solution.py:74
  16.5 0.6 copy-start.19
  16.5 5.0 copy-start.17
  18.3 0.6 copy-start.21
  18.4 3.1 copy-start.18
  20.2 1.2 copy-start.20
  20.2 1.2 copy-start.22
  57.5 48.5 %all-to-all-start.1 = ((bf16[32,128,400]{1,2,0:T(8,128)(2,1)}), bf16[32,128,400]{1,2,0:T(8,128)(2,1)S(1)}, u32[]{:S(2)}, u32[]{:S(2)}) async-start(bf16[32,128,400]{1,2,0:T(8,128)(2,1)} %select_convert_fusion), calls=%async_computation.1 | async-start | bytes 6553600 | tf_op jit(solution)/shard_map/all_to_all | solution.py:77
  86.6 36.2 %copy-start.23 = (pred[256]{0:T(512)(128)(4,1)}, pred[256]{0:T(512)(128)(4,1)S(1)}, u32[]{:S(2)}) copy-start(pred[256]{0:T(512)(128)(4,1)S(1)} %compare_and_fusion.3) | copy-start | bytes 772
  113.4 8.5 %copy-start.2 = (f32[256,200]{0,1:T(8,128)S(1)}, f32[256,200]{0,1:T(8,128)}, u32[]{:S(2)}) copy-start(f32[256,200]{0,1:T(8,128)} %copy.86) | copy-start | bytes 614404
  124.4 8.9 %copy-start.8 = (bf16[256,400]{0,1:T(8,128)(2,1)}, bf16[256,400]{0,1:T(8,128)(2,1)S(1)}, u32[]{:S(2)}) copy-start(bf16[256,400]{0,1:T(8,128)(2,1)S(1)} %get-tuple-element.28) | copy-start | bytes 614404
  132.4 0.9 copy-start.24
  133.3 0.8 copy-start.11
  134.1 10.1 %copy-start.25 = (pred[256]{0:T(512)(128)(4,1)S(1)}, pred[256]{0:T(512)(128)(4,1)}, u32[]{:S(2)}) copy-start(pred[256]{0:T(512)(128)(4,1)} %compare_and_fusion.8) | copy-start | bytes 772
  144.1 1.9 copy-start.3
  153.5 1.9 copy-start.4
  153.5 1.9 copy-start.10
  155.3 2.1 copy-start.13
  155.3 2.1 copy-start.9
  155.3 2.1 copy-start.12
  157.4 3.5 copy-start.6
  157.4 3.5 copy-start.7
  165.6 5.1 copy-start.5
  244.7 5.9 %copy-start.15 = (s32[1,512]{1,0:T(1,128)S(1)}, s32[1,512]{1,0:T(1,128)}, u32[]{:S(2)}) copy-start(s32[1,512]{1,0:T(1,128)} %param.23) | copy-start | bytes 6148
  244.7 49.9 %all-to-all-start.2 = ((bf16[32,128,400]{1,2,0:T(8,128)(2,1)}), bf16[32,128,400]{1,2,0:T(8,128)(2,1)S(1)}, u32[]{:S(2)}, u32[]{:S(2)}) async-start(bf16[32,128,400]{1,2,0:T(8,128)(2,1)} %copy.92), calls=%async_computation.2 | async-start | bytes 6553600 | tf_op jit(solution)/shard_map/all_to_all | solution.py:94
  250.5 188.3 %all-reduce.5.cloned.1.call-start = ((), (), s32[]{:S(2)}) async-start(), calls=%async_computation.4 | async-start | bytes 15204352 | tf_op jit(solution)/shard_map/psum | solution.py:105
  268.0 264.6 %all-reduce.3.cloned.1.call-start = ((), (), s32[]{:S(2)}) async-start(), calls=%async_computation.3 | async-start | bytes 8388608 | tf_op jit(solution)/shard_map/psum | solution.py:103
  330.8 112.4 %copy-start.14 = (f32[7424]{0:T(1024)S(1)}, f32[7424]{0:T(1024)}, u32[]{:S(2)}) copy-start(f32[7424]{0:T(1024)} %param.18) | copy-start | bytes 89092
  438.8 5.3 copy-start.1
  459.4 75.9 %copy-start.16 = (f32[2048]{0:T(1024)S(1)}, f32[2048]{0:T(1024)}, u32[]{:S(2)}) copy-start(f32[2048]{0:T(1024)} %param.16) | copy-start | bytes 24580
  532.6 3.4 copy-start
Sparse Core Ops, SparseCore 0:
  268.2 170.5 all-reduce.4
  441.1 91.4 all-reduce.2
where the time goes:
time: 563 us; the launch traced here: 553 us
  waiting for transfers between devices  221 us (39%)
  other arithmetic  152 us (27%)
  local copies, waits for them, and re-layouts  136 us (24%)
  starting transfers between devices  21.9 us (4%)
  between operations  15 us (3%)
  matrix products  7.76 us (1%)
    psum x1, waiting for transfers between devices, on_device(): rel_total = lax.psum(rel_grad, ('owner', 'dp'))  108 us
    psum x1, waiting for transfers between devices, on_device(): entity_grad = lax.psum(local_sum, 'dp')  73.2 us
    scatter-add x6, other arithmetic, on_device(): slot_grad = slot_grad.at[hs].add(hg).at[ts].add(tg).at[ns].add(ng)  59.8 us
    unnamed x56, local copies, waits for them, and re-layouts  28.5 us
    gather x2, local copies, waits for them, and re-layouts, on_device(): jnp.take(entity_table, asked.reshape(-1), axis=0).astype(jnp.bfloat16)  27.9 us
    scatter-add x1, other arithmetic, on_device(): local_sum = empty.at[asked.reshape(-1)].add(received.reshape(-1, width_two))  27.6 us
    all_to_all x1, waiting for transfers between devices, on_device(): lax.all_to_all(slot_grad.reshape(owners, capacity, width_two).astype(jnp....  26.5 us
    gather x4, local copies, waits for them, and re-layouts, on_device(): negs = jnp.take(pulled, ns, axis=0)  14.9 us
  transfers between devices with their start and end apart: 5, of which 4 were waited for; matrix products, arithmetic and copies ran while one was open for 20% of the time, Pallas kernels for 0%

commit v1 on v0

v1 whole, which is shorter than its diff:
```python
import functools

import jax
import jax.numpy as jnp
from jax import lax
from jax.experimental import pallas as pl
from jax.experimental.pallas import tpu as pltpu
from jax.sharding import PartitionSpec as P

GAMMA = 2.0
RATE = 0.05
LANES = 128
PAIR = 256
BF16 = jnp.bfloat16
F32 = jnp.float32
MESH = pl.DeviceIdType.MESH
VMEM_LIMIT = 60 * 2**20
NT = (((1,), (1,)), ((), ()))
TN = (((0,), (0,)), ((), ()))


def one_hot(rows, base, index):
    at = lax.broadcasted_iota(jnp.int32, (rows, index.shape[1]), 0) + base
    return jnp.where(at == index, 1.0, 0.0).astype(BF16)


def lanes(start, size):
    return pl.ds(pl.multiple_of(start, LANES), size)


def grid_of(owners):
    chips = owners // 2
    along_y = min(4, chips)
    return chips // along_y, along_y


def offset(j, nx, ny):
    dx = j % nx
    return dx, (j // nx + dx) % ny


def partner(me, j, nx, ny, sign):
    chip = me // 2
    dx, dy = offset(j, nx, ny)
    x = (chip // ny + sign * dx + nx) % nx
    y = (chip % ny + sign * dy + ny) % ny
    return (x * ny + y) * 2


def positions(slots, me, nx, ny):
    chip = slots >> 8
    x, y = chip // ny, chip & (ny - 1)
    mine = me // 2
    dx = (mine // ny - x) & (nx - 1)
    dy = (mine % ny - y) & (ny - 1)
    j = ((dy - dx) & (ny - 1)) * nx + dx
    return j * PAIR + (slots & (PAIR - 1))


def as_column(row):
    return jnp.broadcast_to(row, (LANES, row.shape[1])).T[:, :1]


def as_row(column):
    return jnp.broadcast_to(column, (column.shape[0], LANES)).T[:1, :]


def greet(me, owners, dp_me, dps):
    barrier = pltpu.get_barrier_semaphore()

    def hello(k, _):
        pl.semaphore_signal(
            barrier, inc=1, device_id={"owner": (me + k) % owners}, device_id_type=MESH
        )
        return 0

    lax.fori_loop(1, owners, hello, 0)
    for k in range(1, dps):
        pl.semaphore_signal(
            barrier, inc=1, device_id={"dp": (dp_me + k) % dps}, device_id_type=MESH
        )
    pl.semaphore_wait(barrier, owners - 1 + dps - 1)


def block_grads(b, group, neg, used, cosine, sine, grads, phase_grads):
    triples = 2 * group
    cols = lanes(b * group, group)
    tail_cols = lanes(triples + b * group, group)
    neg_cols = lanes(2 * triples + b * neg, neg)
    cos, sin = cosine[:, cols], sine[:, cols]
    width = cos.shape[0]
    heads = used[:, cols].astype(F32)
    head_re, head_im = heads[:width], heads[width:]
    rot_re = head_re * cos - head_im * sin
    rot_im = head_re * sin + head_im * cos
    rotated = jnp.concatenate([rot_re, rot_im], 0)
    diff = rotated - used[:, tail_cols].astype(F32)
    pos_score = GAMMA - jnp.sum(diff * diff, 0, keepdims=True)
    rot_half = rotated.astype(BF16)
    rot_wide = rot_half.astype(F32)
    negs = used[:, neg_cols]
    neg_wide = negs.astype(F32)
    row_norm = as_column(jnp.sum(rot_wide * rot_wide, 0, keepdims=True))
    neg_norm = jnp.sum(neg_wide * neg_wide, 0, keepdims=True)
    cross = lax.dot_general(rot_half, negs, TN, preferred_element_type=F32)
    neg_score = GAMMA - (row_norm + neg_norm - 2.0 * cross)
    weight = jax.nn.sigmoid(neg_score) * (1.0 / neg)
    weight_half = weight.astype(BF16)
    diff_grad = (2.0 * jax.nn.sigmoid(-pos_score)) * diff
    row_sum = as_row(jnp.sum(weight, 1, keepdims=True))
    col_sum = jnp.sum(weight, 0, keepdims=True)
    rot_grad = (
        diff_grad
        - (2.0 * row_sum) * rot_wide
        + 2.0 * lax.dot_general(negs, weight_half, NT, preferred_element_type=F32)
    )
    grads[:, neg_cols] = (
        2.0 * jnp.dot(rot_half, weight_half, preferred_element_type=F32)
        - (2.0 * col_sum) * neg_wide
    ).astype(BF16)
    grads[:, tail_cols] = (-diff_grad).astype(BF16)
    grad_re, grad_im = rot_grad[:width], rot_grad[width:]
    phase_grads[:, cols] = grad_im * rot_re - grad_re * rot_im
    grads[:, cols] = jnp.concatenate(
        [grad_re * cos + grad_im * sin, grad_im * cos - grad_re * sin], 0
    ).astype(BF16)


def pull_kernel(
    owners, group, neg,
    table_hbm, phase_hbm, requests, slots, relation,
    grads, rel_out, asked_out,
    table, phase, table_half, asked, sent, pulled, used, theta, cosine, sine, phase_grads,
    load_sems, ask_send, ask_recv, row_send, row_recv,
):
    nx, ny = grid_of(owners)
    chips = nx * ny
    me = lax.axis_index("owner")
    core = me % 2
    load_table = pltpu.make_async_copy(table_hbm, table, load_sems.at[0])
    load_phase = pltpu.make_async_copy(phase_hbm, phase, load_sems.at[1])
    load_table.start()
    load_phase.start()
    greet(me, owners, 0, 1)

    def ask(j, q):
        to = partner(me, j, nx, ny, -1) + q
        return to, pltpu.make_async_remote_copy(
            src_ref=requests.at[to], dst_ref=asked.at[2 * j + core],
            send_sem=ask_send.at[2 * j + q], recv_sem=ask_recv.at[2 * j + core],
            device_id={"owner": to}, device_id_type=MESH,
        )

    def ask_all(j, _):
        for q in range(2):
            to, copy = ask(j, q)

            @pl.when(to != me)
            def _():
                copy.start()

        return 0

    lax.fori_loop(0, chips, ask_all, 0)
    asked[core] = requests[me]
    load_table.wait()
    table_half[...] = table[...].astype(BF16)

    def row_copy(j, q):
        to = partner(me, j, nx, ny, 1) + q
        return to, pltpu.make_async_remote_copy(
            src_ref=sent.at[2 * j + q],
            dst_ref=pulled.at[:, lanes(j * PAIR + core * LANES, LANES)],
            send_sem=row_send.at[2 * j + q], recv_sem=row_recv.at[2 * j + core],
            device_id={"owner": to}, device_id_type=MESH,
        )

    def wait_from(j, sems, buffer_of):
        for q in range(2):
            @pl.when(partner(me, j, nx, ny, -1) + q != me)
            def _():
                buffer_of(j, q, sems.at[2 * j + q])

    def fetch(j, _):
        for q in range(2):
            @pl.when(partner(me, j, nx, ny, 1) + q != me)
            def _():
                pltpu.make_async_copy(
                    asked.at[2 * j + q], asked.at[2 * j + q], ask_recv.at[2 * j + q]
                ).wait()

        wanted = jnp.concatenate([asked[2 * j], asked[2 * j + 1]], 1)
        rows = jnp.dot(
            table_half[...], one_hot(table_half.shape[1], 0, wanted), preferred_element_type=F32
        ).astype(BF16)
        for q in range(2):
            sent[2 * j + q] = rows[:, q * LANES : (q + 1) * LANES]
            to, copy = row_copy(j, q)

            @pl.when(to != me)
            def _():
                copy.start()

        return 0

    lax.fori_loop(0, chips, fetch, 0)
    pulled[:, lanes(core * LANES, LANES)] = sent[core]

    load_phase.wait()
    rel = relation[...]
    nrel = phase.shape[1]
    width = phase.shape[0]

    def phase_part(start, size):
        part = phase[:, lanes(start, size)]
        high = part.astype(BF16).astype(F32)
        both = jnp.concatenate([high, part - high], 0).astype(BF16)
        return jnp.dot(both, one_hot(size, start, rel), preferred_element_type=F32)

    step = 512
    whole = nrel // step
    theta[...] = jnp.zeros_like(theta)

    def add_phase(k, _):
        theta[...] += phase_part(k * step, step)
        return 0

    lax.fori_loop(0, whole, add_phase, 0)
    if nrel % step:
        theta[...] += phase_part(whole * step, nrel % step)
    angle = theta[:width] + theta[width:]
    cosine[...] = jnp.cos(angle)
    sine[...] = jnp.sin(angle)

    place = positions(slots[...], me, nx, ny)
    uses = slots.shape[1]
    half = chips // 2

    def arrived(j, _):
        for q in range(2):
            @pl.when(partner(me, j, nx, ny, -1) + q != me)
            def _():
                spot = pulled.at[:, lanes(j * PAIR + q * LANES, LANES)]
                pltpu.make_async_copy(spot, spot, row_recv.at[2 * j + q]).wait()

        return 0

    tile = 256
    for part in range(2):
        lax.fori_loop(part * half, (part + 1) * half, arrived, 0)
        base = part * half * PAIR
        for t in range(uses // tile):
            cols = slice(t * tile, (t + 1) * tile)
            found = jnp.dot(
                pulled[:, base : base + half * PAIR],
                one_hot(half * PAIR, base, place[:, cols]),
                preferred_element_type=F32,
            ).astype(BF16)
            used[:, cols] = found if part == 0 else used[:, cols] + found

    for b in range(2):
        block_grads(b, group, neg, used, cosine, sine, grads, phase_grads)

    pushed = phase_grads[...].astype(BF16)

    def rel_part(start, size):
        rel_out[:, lanes(start, size)] = lax.dot_general(
            pushed, one_hot(size, start, rel), NT, preferred_element_type=F32
        ).astype(BF16)

    def add_rel(k, _):
        rel_part(k * step, step)
        return 0

    lax.fori_loop(0, whole, add_rel, 0)
    if nrel % step:
        rel_part(whole * step, nrel % step)

    asked_out[...] = asked[...]

    def sends_done(j, _):
        for q in range(2):
            to, first = ask(j, q)
            _, second = row_copy(j, q)

            @pl.when(to != me)
            def _():
                first.wait_send()

            @pl.when(partner(me, j, nx, ny, 1) + q != me)
            def _():
                second.wait_send()

        return 0

    lax.fori_loop(0, chips, sends_done, 0)


def push_kernel(
    owners, dps,
    grads, slots, asked,
    out,
    sent, received, total, shared, from_dp, full,
    row_send, row_recv, dp_send, dp_recv, all_send, all_recv,
):
    nx, ny = grid_of(owners)
    chips = nx * ny
    me = lax.axis_index("owner")
    dp_me = lax.axis_index("dp")
    core = me % 2
    greet(me, owners, dp_me, dps)
    place = positions(slots[...], me, nx, ny)

    def row_copy(j, q):
        to = partner(me, j, nx, ny, -1) + q
        return to, pltpu.make_async_remote_copy(
            src_ref=sent.at[2 * j + q],
            dst_ref=received.at[:, lanes(j * PAIR + core * LANES, LANES)],
            send_sem=row_send.at[2 * j + q], recv_sem=row_recv.at[2 * j + core],
            device_id={"owner": to}, device_id_type=MESH,
        )

    def push(j, _):
        sums = lax.dot_general(
            grads[...], one_hot(PAIR, j * PAIR, place), NT, preferred_element_type=F32
        ).astype(BF16)
        for q in range(2):
            sent[2 * j + q] = sums[:, q * LANES : (q + 1) * LANES]
            to, copy = row_copy(j, q)

            @pl.when(to != me)
            def _():
                copy.start()

        return 0

    lax.fori_loop(0, chips, push, 0)
    received[:, lanes(core * LANES, LANES)] = sent[core]

    def arrived(j, _):
        for q in range(2):
            @pl.when(partner(me, j, nx, ny, 1) + q != me)
            def _():
                spot = received.at[:, lanes(j * PAIR + q * LANES, LANES)]
                pltpu.make_async_copy(spot, spot, row_recv.at[2 * j + q]).wait()

        return 0

    half = chips // 2
    rows = total.shape[1]
    tile = 256
    for part in range(2):
        lax.fori_loop(part * half, (part + 1) * half, arrived, 0)
        span = slice(part * half * PAIR, (part + 1) * half * PAIR)
        for t in range(rows // tile):
            cols = slice(t * tile, (t + 1) * tile)
            added = lax.dot_general(
                received[:, span], one_hot(tile, t * tile, asked[:, span]), NT,
                preferred_element_type=F32,
            )
            if part == 0:
                total[:, cols] = added
            else:
                total[:, cols] += added

    share = rows // dps
    shared[...] = total[...].astype(BF16)

    def to_dp(k):
        to = (dp_me + k) % dps
        return pltpu.make_async_remote_copy(
            src_ref=shared.at[:, lanes(to * share, share)], dst_ref=from_dp.at[k - 1],
            send_sem=dp_send.at[k - 1], recv_sem=dp_recv.at[k - 1],
            device_id={"dp": to}, device_id_type=MESH,
        )

    mine = lanes(dp_me * share, share)

    def to_all(k):
        to = (dp_me + k) % dps
        return pltpu.make_async_remote_copy(
            src_ref=full.at[:, mine], dst_ref=full.at[:, mine],
            send_sem=all_send.at[k - 1], recv_sem=all_recv.at[k - 1],
            device_id={"dp": to}, device_id_type=MESH,
        )

    for k in range(1, dps):
        to_dp(k).start()
    summed = total[:, mine]
    for k in range(1, dps):
        to_dp(k).wait_recv()
        summed += from_dp[k - 1].astype(F32)
    full[:, mine] = summed.astype(BF16)
    for k in range(1, dps):
        to_all(k).start()
    for k in range(1, dps):
        spot = full.at[:, lanes((dp_me - k + dps) % dps * share, share)]
        pltpu.make_async_copy(spot, spot, all_recv.at[k - 1]).wait()
    out[...] = full[...]
    for k in range(1, dps):
        to_dp(k).wait_send()
        to_all(k).wait_send()

    def sends_done(j, _):
        for q in range(2):
            to, copy = row_copy(j, q)

            @pl.when(to != me)
            def _():
                copy.wait_send()

        return 0

    lax.fori_loop(0, chips, sends_done, 0)


def adagrad_kernel(table, state, grad, new_table, new_state):
    g = grad[...].astype(F32)
    fresh = state[...] + jnp.sum(g * g, 0, keepdims=True) * (1.0 / g.shape[0])
    new_state[...] = fresh
    new_table[...] = table[...] - g * (RATE / jnp.sqrt(fresh))


def adagrad(table, state, grad, tile):
    width, rows = table.shape
    wide = pl.BlockSpec((width, tile), lambda i: (0, i))
    thin = pl.BlockSpec((1, tile), lambda i: (0, i))
    new_table, new_state = pl.pallas_call(
        adagrad_kernel,
        grid=(pl.cdiv(rows, tile),),
        out_shape=(
            jax.ShapeDtypeStruct((width, rows), F32),
            jax.ShapeDtypeStruct((1, rows), F32),
        ),
        in_specs=[wide, thin, wide],
        out_specs=(wide, thin),
        compiler_params=pltpu.CompilerParams(vmem_limit_bytes=VMEM_LIMIT),
    )(table, state[None], grad)
    return new_table.T, new_state[0]


VM = pl.BlockSpec(memory_space=pltpu.VMEM)
HBM = pl.BlockSpec(memory_space=pl.ANY)


def on_device(
    entity_table, entity_state, phase_table, phase_state,
    pull_rows, head_slot, tail_slot, neg_slot, relation,
):
    owners, dps = lax.axis_size("owner"), lax.axis_size("dp")
    table, phase = entity_table.T, phase_table.T
    width, rows = table.shape
    narrow, nrel = phase.shape
    triples = head_slot.shape[1]
    neg = neg_slot.shape[2]
    slots = jnp.concatenate([head_slot, tail_slot, neg_slot.reshape(1, -1)], 1)
    uses = slots.shape[1]
    pulls = owners * LANES
    requests = pull_rows.reshape(owners, 1, LANES)
    dma = pltpu.SemaphoreType.DMA
    grads, rel_grad, asked = pl.pallas_call(
        functools.partial(pull_kernel, owners, triples // 2, neg),
        out_shape=(
            jax.ShapeDtypeStruct((width, uses), BF16),
            jax.ShapeDtypeStruct((narrow, nrel), BF16),
            jax.ShapeDtypeStruct((owners, 1, LANES), jnp.int32),
        ),
        in_specs=[HBM, HBM, VM, VM, VM],
        out_specs=(VM, VM, VM),
        scratch_shapes=[
            pltpu.VMEM((width, rows), F32),
            pltpu.VMEM((narrow, nrel), F32),
            pltpu.VMEM((width, rows), BF16),
            pltpu.VMEM((owners, 1, LANES), jnp.int32),
            pltpu.VMEM((owners, width, LANES), BF16),
            pltpu.VMEM((width, pulls), BF16),
            pltpu.VMEM((width, uses), BF16),
            pltpu.VMEM((width, triples), F32),
            pltpu.VMEM((narrow, triples), F32),
            pltpu.VMEM((narrow, triples), F32),
            pltpu.VMEM((narrow, triples), F32),
            dma((2,)), dma((owners,)), dma((owners,)), dma((owners,)), dma((owners,)),
        ],
        compiler_params=pltpu.CompilerParams(
            collective_id=0, has_side_effects=True, vmem_limit_bytes=VMEM_LIMIT
        ),
        name="pull",
    )(table, phase, requests, slots, relation)
    rel_total = lax.psum(rel_grad, ("owner", "dp"))
    grad = pl.pallas_call(
        functools.partial(push_kernel, owners, dps),
        out_shape=jax.ShapeDtypeStruct((width, rows), BF16),
        in_specs=[VM, VM, VM],
        out_specs=VM,
        scratch_shapes=[
            pltpu.VMEM((owners, width, LANES), BF16),
            pltpu.VMEM((width, pulls), BF16),
            pltpu.VMEM((width, rows), F32),
            pltpu.VMEM((width, rows), BF16),
            pltpu.VMEM((dps - 1, width, rows // dps), BF16),
            pltpu.VMEM((width, rows), BF16),
            dma((owners,)), dma((owners,)),
            dma((dps - 1,)), dma((dps - 1,)), dma((dps - 1,)), dma((dps - 1,)),
        ],
        compiler_params=pltpu.CompilerParams(
            collective_id=1, has_side_effects=True, vmem_limit_bytes=VMEM_LIMIT
        ),
        name="push",
    )(grads, slots, asked.reshape(1, pulls))
    new_entity, new_entity_state = adagrad(table, entity_state, grad, 512)
    new_phase, new_phase_state = adagrad(phase, phase_state, rel_total, 1024)
    return (new_entity, new_entity_state, new_phase, new_phase_state)


def solution(mesh):
    placed = (
        P("owner", None),
        P("owner"),
        P(),
        P(),
        P(("owner", "dp"), None, None),
        P(("owner", "dp"), None),
        P(("owner", "dp"), None),
        P(("owner", "dp"), None, None),
        P(("owner", "dp"), None),
    )
    return jax.shard_map(
        on_device,
        mesh=mesh,
        in_specs=placed,
        out_specs=(P("owner", None), P("owner"), P(), P()),
        check_vma=False,
    )
```

time: 563 us -> 304 us (0.54); the launches traced: 553 us -> 303 us
  Pallas kernels: 0 us -> 184 us
  other arithmetic: 152 us -> 1.44 us
  local copies, waits for them, and re-layouts: 136 us -> 3.32 us
  waiting for transfers between devices: 221 us -> 100 us
  starting transfers between devices: 21.9 us -> 0.04 us
  matrix products: 7.76 us -> 0 us
    pallas_call x0 -> x4, Pallas kernels: none -> 184 us  [the longest x1 97.2 us: on_device(): pl.pallas_call(functools.partial(push_kernel, owners, dps), out_shape=jax...]
    scatter-add x9 -> x0, other arithmetic: 101 us -> none  [the longest x6 59.8 us: on_device(): slot_grad = slot_grad.at[hs].add(hg).at[ts].add(tg).at[ns].add(ng)]
    psum x1 -> x0, waiting for transfers between devices: 73.2 us -> none  [on_device(): entity_grad = lax.psum(local_sum, 'dp')]
    gather x18 -> x0, local copies, waits for them, and re-layouts: 70.8 us -> none  [the longest x2 27.9 us: on_device(): jnp.take(entity_table, asked.reshape(-1), axis=0).astype(jnp.bfloat16)]
    all_to_all x3 -> x0, waiting for transfers between devices: 39.8 us -> none  [the longest x1 26.5 us: on_device(): lax.all_to_all(slot_grad.reshape(owners, capacity, width_two).astype(jnp....]
    unnamed x56 -> x7, local copies, waits for them, and re-layouts: 28.5 us -> 2.68 us
    all_to_all x3 -> x0, starting transfers between devices: 21.8 us -> none  [the longest x1 8.6 us: on_device(): lax.all_to_all(requests, 'owner', split_axis=0, concat_axis=0, tiled=True)]
    sub x4 -> x0, other arithmetic: 13.5 us -> none  [the longest x2 11.9 us: adagrad(): return (table - RATE * grad / jnp.sqrt(new_state)[:, None], new_state)]
  transfers between devices with their start and end apart: 5 -> 1, of which waited for: 4 -> 1; matrix products, arithmetic and copies ran while one was open for 20% -> 0% of each run, Pallas kernels for 0% -> 34%
where the time goes in v1:
time: 304 us; the launch traced here: 303 us
  Pallas kernels  184 us (61%)
  waiting for transfers between devices  100 us (33%)
  between operations  14.1 us (5%)
  local copies, waits for them, and re-layouts  3.32 us (1%)
    psum x1, waiting for transfers between devices, on_device(): rel_total = lax.psum(rel_grad, ('owner', 'dp'))  100 us
    pallas_call x1, Pallas kernels, on_device(): pl.pallas_call(functools.partial(push_kernel, owners, dps), out_shape=jax...  97.2 us
    pallas_call x1, Pallas kernels, on_device(): pl.pallas_call(functools.partial(pull_kernel, owners, triples // 2, neg),...  73.1 us
    pallas_call x2, Pallas kernels, adagrad(): pl.pallas_call(adagrad_kernel, grid=(pl.cdiv(rows, tile),), out_shape=(ja...  13.7 us
  transfers between devices with their start and end apart: 1, of which 1 were waited for; matrix products, arithmetic and copies ran while one was open for 0% of the time, Pallas kernels for 34%

profile of v1, /device:TPU:1, one launch (start us, length us, event | category | flops | bytes accessed | tf_op | source)
XLA Modules:
  0.0 303.4 jit_solution(12375921718821665003)
XLA Ops:
  7.2 0.0 all-reduce.2.cloned.1.call-start
  7.2 0.7 copy.13
  7.9 0.7 constant_dynamic-update-slice_fusion.2
  8.6 0.7 constant_dynamic-update-slice_fusion.1
  9.3 0.0 copy-start
  9.3 0.6 copy-done
  9.9 0.0 copy-start.1
  9.9 73.1 %pull.1 = (bf16[400,3072]{1,0:T(8,128)(2,1)}, bf16[200,7424]{1,0:T(8,128)(2,1)}, s32[32,1,128]{2,1,0:T(1,128)}) custom-call(f32[400,2048]{1,0:T(8,128)} %bitcast.12, f32[200,7424]{1,0:T(8,128)} %bitcast.10, s32[32,1,128]{2,1,0:T(1,128)} %bitcast.15, s32[1,3072]{1,0:T(1,128)} %copy-done, s32[1,512]{1,0:T(1,128)} %relation.1), custom_call_target="tpu_custom_call" | custom-call | tf_op jit(solution)/shard_map/pull/pallas_call | solution.py:461
  83.0 0.0 all-reduce.2.cloned.1.call-update
  83.0 0.0 copy-done.1
  83.0 0.6 broadcast_in_dim.7.state
  83.7 97.2 %push.1.grad = bf16[400,2048]{1,0:T(8,128)(2,1)} custom-call(bf16[400,3072]{1,0:T(8,128)(2,1)} %get-tuple-element.11.grads, s32[1,3072]{1,0:T(1,128)} %copy-done, s32[1,4096]{1,0:T(1,128)} %bitcast.16), custom_call_target="tpu_custom_call" | custom-call | tf_op jit(solution)/shard_map/push/pallas_call | solution.py:490
  180.9 4.9 %shard_map.120 = (f32[400,2048]{1,0:T(8,128)}, f32[1,2048]{1,0:T(1,128)}) custom-call(f32[400,2048]{1,0:T(8,128)} %bitcast.13, f32[1,2048]{1,0:T(1,128)} %bitcast.17, bf16[400,2048]{1,0:T(8,128)(2,1)} %push.1.grad), custom_call_target="tpu_custom_call" | custom-call | tf_op jit(solution)/shard_map/pallas_call | solution.py:428
  185.8 100.5 %all-reduce.2.cloned.1.call-done.grad = bf16[200,7424]{1,0:T(8,128)(2,1)} async-done(((bf16[200,7424]{1,0:T(8,128)(2,1)}), bf16[200,7424]{1,0:T(8,128)(2,1)}) %all-reduce.2.cloned.1.call-update) | async-done | bytes 2969616 | tf_op jit(solution)/shard_map/psum | solution.py:489
  286.3 8.8 %shard_map.121 = (f32[200,7424]{1,0:T(8,128)}, f32[1,7424]{1,0:T(1,128)}) custom-call(f32[200,7424]{1,0:T(8,128)} %bitcast.11, f32[1,7424]{1,0:T(1,128)} %broadcast_in_dim.7.state, bf16[200,7424]{1,0:T(8,128)(2,1)} %all-reduce.2.cloned.1.call-done.grad), custom_call_target="tpu_custom_call" | custom-call | tf_op jit(solution)/shard_map/pallas_call | solution.py:428
  295.1 1.4 reduce
  (1 shorter events, 0.0 us)
Async XLA Ops:
  7.2 279.1 %all-reduce.2.cloned.1.call-start = ((), (), s32[]{:S(2)}) async-start(), calls=%async_computation | async-start | bytes 5939200 | tf_op jit(solution)/shard_map/psum | solution.py:489
  9.3 0.6 copy-start
  9.9 73.1 %copy-start.1 = (f32[7424]{0:T(1024)S(1)}, f32[7424]{0:T(1024)}, u32[]{:S(2)}) copy-start(f32[7424]{0:T(1024)} %param.12) | copy-start | bytes 89092
Sparse Core Ops, SparseCore 0:
  83.1 203.1 all-reduce.1

commit v2 on v1

v2 whole, which is shorter than its diff:
```python
import functools

import jax
import jax.numpy as jnp
from jax import lax
from jax.experimental import pallas as pl
from jax.experimental.pallas import tpu as pltpu
from jax.sharding import PartitionSpec as P

GAMMA = 2.0
RATE = 0.05
LANES = 128
PAIR = 256
BF16 = jnp.bfloat16
F32 = jnp.float32
MESH = pl.DeviceIdType.MESH
VMEM_LIMIT = 60 * 2**20
NT = (((1,), (1,)), ((), ()))
TN = (((0,), (0,)), ((), ()))


def one_hot(rows, base, index):
    at = lax.broadcasted_iota(jnp.int32, (rows, index.shape[1]), 0) + base
    return jnp.where(at == index, 1.0, 0.0).astype(BF16)


def lanes(start, size):
    return pl.ds(pl.multiple_of(start, LANES), size)


def grid_of(owners):
    chips = owners // 2
    along_y = min(4, chips)
    return chips // along_y, along_y


def offset(j, nx, ny):
    dx = j % nx
    return dx, (j // nx + dx) % ny


def partner(me, j, nx, ny, sign):
    chip = me // 2
    dx, dy = offset(j, nx, ny)
    x = (chip // ny + sign * dx + nx) % nx
    y = (chip % ny + sign * dy + ny) % ny
    return (x * ny + y) * 2


def positions(slots, me, nx, ny):
    chip = slots >> 8
    x, y = chip // ny, chip & (ny - 1)
    mine = me // 2
    dx = (mine // ny - x) & (nx - 1)
    dy = (mine % ny - y) & (ny - 1)
    j = ((dy - dx) & (ny - 1)) * nx + dx
    return j * PAIR + (slots & (PAIR - 1))


def as_column(row):
    return jnp.broadcast_to(row, (LANES, row.shape[1])).T[:, :1]


def as_row(column):
    return jnp.broadcast_to(column, (column.shape[0], LANES)).T[:1, :]


def greet(me, owners, dp_me, dps):
    barrier = pltpu.get_barrier_semaphore()

    def hello(k, _):
        pl.semaphore_signal(
            barrier, inc=1, device_id={"owner": (me + k) % owners}, device_id_type=MESH
        )
        return 0

    lax.fori_loop(1, owners, hello, 0)
    for k in range(1, dps):
        pl.semaphore_signal(
            barrier, inc=1, device_id={"dp": (dp_me + k) % dps}, device_id_type=MESH
        )
    pl.semaphore_wait(barrier, owners - 1 + dps - 1)


def block_grads(b, group, neg, used, cosine, sine, grads, phase_grads):
    triples = 2 * group
    cols = lanes(b * group, group)
    tail_cols = lanes(triples + b * group, group)
    neg_cols = lanes(2 * triples + b * neg, neg)
    cos, sin = cosine[:, cols], sine[:, cols]
    width = cos.shape[0]
    heads = used[:, cols].astype(F32)
    head_re, head_im = heads[:width], heads[width:]
    rot_re = head_re * cos - head_im * sin
    rot_im = head_re * sin + head_im * cos
    rotated = jnp.concatenate([rot_re, rot_im], 0)
    diff = rotated - used[:, tail_cols].astype(F32)
    pos_score = GAMMA - jnp.sum(diff * diff, 0, keepdims=True)
    rot_half = rotated.astype(BF16)
    rot_wide = rot_half.astype(F32)
    negs = used[:, neg_cols]
    neg_wide = negs.astype(F32)
    row_norm = as_column(jnp.sum(rot_wide * rot_wide, 0, keepdims=True))
    neg_norm = jnp.sum(neg_wide * neg_wide, 0, keepdims=True)
    cross = lax.dot_general(rot_half, negs, TN, preferred_element_type=F32)
    neg_score = GAMMA - (row_norm + neg_norm - 2.0 * cross)
    weight = jax.nn.sigmoid(neg_score) * (1.0 / neg)
    weight_half = weight.astype(BF16)
    diff_grad = (2.0 * jax.nn.sigmoid(-pos_score)) * diff
    row_sum = as_row(jnp.sum(weight, 1, keepdims=True))
    col_sum = jnp.sum(weight, 0, keepdims=True)
    rot_grad = (
        diff_grad
        - (2.0 * row_sum) * rot_wide
        + 2.0 * lax.dot_general(negs, weight_half, NT, preferred_element_type=F32)
    )
    grads[:, neg_cols] = (
        2.0 * jnp.dot(rot_half, weight_half, preferred_element_type=F32)
        - (2.0 * col_sum) * neg_wide
    ).astype(BF16)
    grads[:, tail_cols] = (-diff_grad).astype(BF16)
    grad_re, grad_im = rot_grad[:width], rot_grad[width:]
    phase_grads[:width, cols] = grad_im * rot_re - grad_re * rot_im
    grads[:, cols] = jnp.concatenate(
        [grad_re * cos + grad_im * sin, grad_im * cos - grad_re * sin], 0
    ).astype(BF16)


def arrive(ref, sem):
    pltpu.make_async_copy(ref, ref, sem).wait()


class RingSum:
    def __init__(self, dp_me, piece, landing, send, recv):
        self.piece, self.landing, self.send, self.recv = piece, landing, send, recv
        self.me, self.right, self.left = dp_me, (dp_me + 1) % 4, (dp_me + 3) % 4
        self.opposite = (dp_me + 2) % 4

    def copy(self, src, slot, to):
        return pltpu.make_async_remote_copy(
            src_ref=src, dst_ref=self.landing[slot],
            send_sem=self.send.at[slot], recv_sem=self.recv.at[slot],
            device_id={"dp": to}, device_id_type=MESH,
        )

    def part(self, slot):
        z, h, to = (
            (self.opposite, 0, self.right),
            (self.opposite, 1, self.left),
            (self.right, 1, self.right),
            (self.left, 0, self.left),
            (self.right, 0, self.right),
            (self.left, 1, self.left),
        )[slot]
        return self.copy(self.piece(z, h), slot, to)

    def begin(self):
        for slot in range(4):
            self.part(slot).start()

    def relay(self):
        for slot, z, h in ((0, self.right, 0), (1, self.left, 1)):
            arrive(self.landing[slot], self.recv.at[slot])
            spot = self.piece(z, h)
            spot[...] = (spot[...].astype(F32) + self.landing[slot][...].astype(F32)).astype(BF16)
            self.part(4 + slot).start()

    def finish(self, h):
        slots = (4, 3) if h == 0 else (5, 2)
        for slot in slots:
            arrive(self.landing[slot], self.recv.at[slot])
        return self.landing[slots[0]][...].astype(F32) + self.landing[slots[1]][...].astype(F32)

    def drain(self):
        for slot in range(6):
            self.part(slot).wait_send()


class RingGather:
    def __init__(self, dp_me, piece, send, recv):
        self.piece, self.send, self.recv = piece, send, recv
        self.me, self.right, self.left = dp_me, (dp_me + 1) % 4, (dp_me + 3) % 4
        self.opposite = (dp_me + 2) % 4

    def part(self, slot):
        z, h, to = (
            (self.me, 0, self.right),
            (self.me, 1, self.left),
            (self.me, 1, self.right),
            (self.me, 0, self.left),
            (self.left, 0, self.right),
            (self.right, 1, self.left),
        )[slot]
        return pltpu.make_async_remote_copy(
            src_ref=self.piece(z, h), dst_ref=self.piece(z, h),
            send_sem=self.send.at[slot], recv_sem=self.recv.at[slot],
            device_id={"dp": to}, device_id_type=MESH,
        )

    def begin(self):
        for slot in range(4):
            self.part(slot).start()

    def relay(self):
        arrive(self.piece(self.left, 0), self.recv.at[0])
        self.part(4).start()
        arrive(self.piece(self.right, 1), self.recv.at[1])
        self.part(5).start()

    def finish(self):
        arrive(self.piece(self.left, 1), self.recv.at[2])
        arrive(self.piece(self.right, 0), self.recv.at[3])
        arrive(self.piece(self.opposite, 0), self.recv.at[4])
        arrive(self.piece(self.opposite, 1), self.recv.at[5])

    def drain(self):
        for slot in range(6):
            self.part(slot).wait_send()


def step_kernel(
    owners, group, neg,
    table_hbm, phase_hbm, requests, slots, relation,
    grad_out, rel_out,
    table, phase, table_half, asked, asked_row, sent, pulled, used, grads,
    theta, cosine, sine, phase_grads,
    received, total, shared, dp_in, full,
    rel, core_in, ring_in, plane_in, rel_sum,
    load_sems, ask_send, ask_recv, row_send, row_recv, back_send, back_recv,
    dp_send, dp_recv, all_send, all_recv,
    core_send, core_recv, ring_send, ring_recv, plane_send, plane_recv,
    spread_send, spread_recv, gather_send, gather_recv,
):
    nx, ny = grid_of(owners)
    chips = nx * ny
    me = lax.axis_index("owner")
    dp_me = lax.axis_index("dp")
    core = me % 2
    load_table = pltpu.make_async_copy(table_hbm, table, load_sems.at[0])
    load_phase = pltpu.make_async_copy(phase_hbm, phase, load_sems.at[1])
    load_table.start()
    load_phase.start()
    greet(me, owners, dp_me, 4)

    def each_core(j, sign, act):
        for q in range(2):
            to = partner(me, j, nx, ny, sign) + q

            @pl.when(to != me)
            def _():
                act(q, to)

    def over_chips(low, high, sign, act):
        def body(j, _):
            each_core(j, sign, functools.partial(act, j))
            return 0

        lax.fori_loop(low, high, body, 0)

    def ask(j, q, to):
        return pltpu.make_async_remote_copy(
            src_ref=requests.at[to], dst_ref=asked.at[2 * j + core],
            send_sem=ask_send.at[2 * j + q], recv_sem=ask_recv.at[2 * j + core],
            device_id={"owner": to}, device_id_type=MESH,
        )

    over_chips(0, chips, -1, lambda j, q, to: ask(j, q, to).start())
    asked[core] = requests[me]
    load_table.wait()
    table_half[...] = table[...].astype(BF16)

    def row_copy(j, q, to):
        return pltpu.make_async_remote_copy(
            src_ref=sent.at[2 * j + q],
            dst_ref=pulled.at[:, lanes(j * PAIR + core * LANES, LANES)],
            send_sem=row_send.at[2 * j + q], recv_sem=row_recv.at[2 * j + core],
            device_id={"owner": to}, device_id_type=MESH,
        )

    def fetch(j, _):
        each_core(j, 1, lambda q, to: arrive(asked.at[2 * j + q], ask_recv.at[2 * j + q]))
        wanted = jnp.concatenate([asked[2 * j], asked[2 * j + 1]], 1)
        asked_row[:, lanes(j * PAIR, PAIR)] = wanted
        rows = jnp.dot(
            table_half[...], one_hot(table_half.shape[1], 0, wanted), preferred_element_type=F32
        ).astype(BF16)
        for q in range(2):
            sent[2 * j + q] = rows[:, q * LANES : (q + 1) * LANES]
        each_core(j, 1, lambda q, to: row_copy(j, q, to).start())
        return 0

    lax.fori_loop(0, chips, fetch, 0)
    pulled[:, lanes(core * LANES, LANES)] = sent[core]

    load_phase.wait()
    rel_index = relation[...]
    nrel = phase.shape[1]
    width = phase.shape[0]
    step = 512
    whole = nrel // step

    def phase_part(start, size):
        part = phase[:, lanes(start, size)]
        high = part.astype(BF16).astype(F32)
        both = jnp.concatenate([high, part - high], 0).astype(BF16)
        return jnp.dot(both, one_hot(size, start, rel_index), preferred_element_type=F32)

    theta[...] = jnp.zeros_like(theta)

    def add_phase(k, _):
        theta[...] += phase_part(k * step, step)
        return 0

    lax.fori_loop(0, whole, add_phase, 0)
    if nrel % step:
        theta[...] += phase_part(whole * step, nrel % step)
    angle = theta[:width] + theta[width:]
    cosine[...] = jnp.cos(angle)
    sine[...] = jnp.sin(angle)

    place = positions(slots[...], me, nx, ny)
    uses = slots.shape[1]
    tile = 256
    cuts = (0, chips // 2, chips - chips // 4, chips)
    for low, high in zip(cuts[:-1], cuts[1:]):
        if low == high:
            continue
        over_chips(
            low, high, -1,
            lambda j, q, to: arrive(
                pulled.at[:, lanes(j * PAIR + q * LANES, LANES)], row_recv.at[2 * j + q]
            ),
        )
        for t in range(uses // tile):
            cols = slice(t * tile, (t + 1) * tile)
            found = jnp.dot(
                pulled[:, low * PAIR : high * PAIR],
                one_hot((high - low) * PAIR, low * PAIR, place[:, cols]),
                preferred_element_type=F32,
            ).astype(BF16)
            used[:, cols] = found if low == 0 else used[:, cols] + found

    phase_grads[width:] = jnp.zeros_like(phase_grads[width:])
    for b in range(2):
        block_grads(b, group, neg, used, cosine, sine, grads, phase_grads)

    pushed = phase_grads[...].astype(BF16)
    per_tile = pushed.shape[0] // 16
    tiles = nrel // LANES

    def rel_part(start_tile, count):
        part = lax.dot_general(
            pushed, one_hot(count * LANES, start_tile * LANES, rel_index), NT,
            preferred_element_type=F32,
        ).astype(BF16)
        for i in range(count):
            rel[pl.ds((start_tile + i) * per_tile, per_tile)] = part[
                :, i * LANES : (i + 1) * LANES
            ].reshape(per_tile, 16, LANES)

    def add_rel(k, _):
        rel_part(k * (step // LANES), step // LANES)
        return 0

    lax.fori_loop(0, whole, add_rel, 0)
    if nrel % step:
        rel_part(whole * (step // LANES), (nrel % step) // LANES)
    units = rel.shape[0]
    if units > tiles * per_tile:
        rel[tiles * per_tile :] = jnp.zeros_like(rel[tiles * per_tile :])

    by_core, by_dp, by_chip = units // 2, units // 8, units // 8 // chips
    core_base = core * by_core
    dp_base = core_base + dp_me * by_dp
    my_base = dp_base + me // 2 * by_chip
    sibling = me + 1 - 2 * core
    swap = pltpu.make_async_remote_copy(
        src_ref=rel.at[pl.ds((1 - core) * by_core, by_core)], dst_ref=core_in,
        send_sem=core_send.at[0], recv_sem=core_recv.at[0],
        device_id={"owner": sibling}, device_id_type=MESH,
    )
    swap.start()
    ring = RingSum(
        dp_me,
        lambda z, h: rel.at[pl.ds(core_base + z * by_dp + h * (by_dp // 2), by_dp // 2)],
        [ring_in.at[i] for i in range(6)], ring_send, ring_recv,
    )

    def plane_copy(j):
        to = partner(me, j, nx, ny, 1) + core
        return pltpu.make_async_remote_copy(
            src_ref=rel.at[pl.ds(dp_base + to // 2 * by_chip, by_chip)], dst_ref=plane_in.at[j],
            send_sem=plane_send.at[j], recv_sem=plane_recv.at[j],
            device_id={"owner": to}, device_id_type=MESH,
        )

    def spread_copy(j):
        to = partner(me, j, nx, ny, 1) + core
        mine = rel_sum.at[pl.ds(my_base, by_chip)]
        return pltpu.make_async_remote_copy(
            src_ref=mine, dst_ref=mine,
            send_sem=spread_send.at[j], recv_sem=spread_recv.at[j],
            device_id={"owner": to}, device_id_type=MESH,
        )

    def loop(low, high, act):
        def body(j, _):
            act(j)
            return 0

        lax.fori_loop(low, high, body, 0)

    rel_ring = RingGather(
        dp_me,
        lambda z, h: rel_sum.at[pl.ds(core_base + z * by_dp + h * (by_dp // 2), by_dp // 2)],
        gather_send, gather_recv,
    )
    share_core = rel_sum.at[pl.ds(core_base, by_core)]
    give = pltpu.make_async_remote_copy(
        src_ref=share_core, dst_ref=share_core,
        send_sem=core_send.at[1], recv_sem=core_recv.at[1],
        device_id={"owner": sibling}, device_id_type=MESH,
    )

    over_chips(0, chips, 1, lambda j, q, to: row_copy(j, q, to).wait_send())

    def back_copy(j, q, to):
        return pltpu.make_async_remote_copy(
            src_ref=sent.at[2 * j + q],
            dst_ref=received.at[:, lanes(j * PAIR + core * LANES, LANES)],
            send_sem=back_send.at[2 * j + q], recv_sem=back_recv.at[2 * j + core],
            device_id={"owner": to}, device_id_type=MESH,
        )

    def push(j, _):
        sums = lax.dot_general(
            grads[...], one_hot(PAIR, j * PAIR, place), NT, preferred_element_type=F32
        ).astype(BF16)
        for q in range(2):
            sent[2 * j + q] = sums[:, q * LANES : (q + 1) * LANES]
        each_core(j, -1, lambda q, to: back_copy(j, q, to).start())
        return 0

    first = min(4, chips)
    later = max(first, chips - 2)
    lax.fori_loop(0, first, push, 0)
    received[:, lanes(core * LANES, LANES)] = sent[core]
    arrive(core_in, core_recv.at[0])
    own_core = rel.at[pl.ds(core_base, by_core)]
    own_core[...] = (own_core[...].astype(F32) + core_in[...].astype(F32)).astype(BF16)
    ring.begin()
    lax.fori_loop(first, later, push, 0)
    ring.relay()
    lax.fori_loop(later, chips, push, 0)
    for h in range(2):
        spot = ring.piece(dp_me, h)
        spot[...] = (spot[...].astype(F32) + ring.finish(h)).astype(BF16)
    loop(1, chips, lambda j: plane_copy(j).start())

    half = chips // 2 if chips > 1 else chips
    rows = total.shape[1]

    def scatter(low, high):
        over_chips(
            low, high, 1,
            lambda j, q, to: arrive(
                received.at[:, lanes(j * PAIR + q * LANES, LANES)], back_recv.at[2 * j + q]
            ),
        )
        span = slice(low * PAIR, high * PAIR)
        for t in range(rows // tile):
            cols = slice(t * tile, (t + 1) * tile)
            added = lax.dot_general(
                received[:, span], one_hot(tile, t * tile, asked_row[:, span]), NT,
                preferred_element_type=F32,
            )
            if low == 0:
                total[:, cols] = added
            else:
                total[:, cols] += added

    scatter(0, half)
    mine = rel.at[pl.ds(my_base, by_chip)][...].astype(F32)

    def add_plane(j, value):
        arrive(plane_in.at[j], plane_recv.at[j])
        return value + plane_in[j].astype(F32)

    rel_sum[pl.ds(my_base, by_chip)] = lax.fori_loop(1, chips, add_plane, mine).astype(BF16)
    loop(1, chips, lambda j: spread_copy(j).start())

    def spread_in(j):
        chip = partner(me, j, nx, ny, -1) // 2
        arrive(rel_sum.at[pl.ds(dp_base + chip * by_chip, by_chip)], spread_recv.at[j])

    loop(1, chips, spread_in)
    rel_ring.begin()
    if half < chips:
        scatter(half, chips)

    share = rows // 4
    split = total.shape[0] // 32 * 16
    shared[...] = total[...].astype(BF16)

    def piece_of(ref):
        def piece(z, h):
            features = pl.ds(0, split) if h == 0 else pl.ds(split, ref.shape[0] - split)
            return ref.at[features, lanes(z * share, share)]

        return piece

    big = shared.shape[0] - split
    dp_ring = RingSum(
        dp_me, piece_of(shared),
        [dp_in.at[i, pl.ds(0, big if i in (1, 2, 5) else split)] for i in range(6)],
        dp_send, dp_recv,
    )
    dp_ring.begin()
    rel_ring.relay()
    dp_ring.relay()
    rel_ring.finish()
    give.start()
    all_ring = RingGather(dp_me, piece_of(full), all_send, all_recv)
    for h in range(2):
        own = total.at[pl.ds(0, split) if h == 0 else pl.ds(split, big), lanes(dp_me * share, share)]
        all_ring.piece(dp_me, h)[...] = (own[...] + dp_ring.finish(h)).astype(BF16)
    all_ring.begin()
    arrive(rel_sum.at[pl.ds((1 - core) * by_core, by_core)], core_recv.at[1])

    def lay(t):
        rel_out[:, lanes(t * LANES, LANES)] = rel_sum[pl.ds(t * per_tile, per_tile)].reshape(
            per_tile * 16, LANES
        )

    loop(0, tiles, lay)
    all_ring.relay()
    swap.wait_send()
    give.wait_send()
    ring.drain()
    rel_ring.drain()
    dp_ring.drain()
    loop(1, chips, lambda j: plane_copy(j).wait_send())
    loop(1, chips, lambda j: spread_copy(j).wait_send())
    over_chips(0, chips, -1, lambda j, q, to: ask(j, q, to).wait_send())
    over_chips(0, chips, -1, lambda j, q, to: back_copy(j, q, to).wait_send())
    all_ring.finish()
    grad_out[...] = full[...]
    all_ring.drain()


def adagrad_kernel(table, state, grad, new_table, new_state):
    g = grad[: table.shape[0]].astype(F32)
    fresh = state[...] + jnp.sum(g * g, 0, keepdims=True) * (1.0 / g.shape[0])
    new_state[...] = fresh
    new_table[...] = table[...] - g * (RATE / jnp.sqrt(fresh))


def adagrad(table, state, grad, tile):
    width, rows = table.shape
    wide = pl.BlockSpec((width, tile), lambda i: (0, i))
    thin = pl.BlockSpec((1, tile), lambda i: (0, i))
    new_table, new_state = pl.pallas_call(
        adagrad_kernel,
        grid=(pl.cdiv(rows, tile),),
        out_shape=(
            jax.ShapeDtypeStruct((width, rows), F32),
            jax.ShapeDtypeStruct((1, rows), F32),
        ),
        in_specs=[wide, thin, pl.BlockSpec((grad.shape[0], tile), lambda i: (0, i))],
        out_specs=(wide, thin),
        compiler_params=pltpu.CompilerParams(vmem_limit_bytes=VMEM_LIMIT),
    )(table, state[None], grad)
    return new_table.T, new_state.reshape(rows)


VM = pl.BlockSpec(memory_space=pltpu.VMEM)
HBM = pl.BlockSpec(memory_space=pl.ANY)


def on_device(
    entity_table, entity_state, phase_table, phase_state,
    pull_rows, head_slot, tail_slot, neg_slot, relation,
):
    owners, dps = lax.axis_size("owner"), lax.axis_size("dp")
    table, phase = entity_table.T, phase_table.T
    width, rows = table.shape
    narrow, nrel = phase.shape
    triples = head_slot.shape[1]
    neg = neg_slot.shape[2]
    slots = jnp.concatenate([head_slot, tail_slot, neg_slot.reshape(1, -1)], 1)
    uses = slots.shape[1]
    pulls = owners * LANES
    requests = pull_rows.reshape(owners, 1, LANES)
    dma = pltpu.SemaphoreType.DMA
    chips = owners // 2
    padded = -(-narrow // 16) * 16
    units = -(-nrel // LANES * padded // 16 // (16 * chips)) * 16 * chips
    big = width - width // 32 * 16
    grad, rel_total = pl.pallas_call(
        functools.partial(step_kernel, owners, triples // 2, neg),
        out_shape=(
            jax.ShapeDtypeStruct((width, rows), BF16),
            jax.ShapeDtypeStruct((padded, nrel), BF16),
        ),
        in_specs=[HBM, HBM, VM, VM, VM],
        out_specs=(VM, VM),
        scratch_shapes=[
            pltpu.VMEM((width, rows), F32),
            pltpu.VMEM((narrow, nrel), F32),
            pltpu.VMEM((width, rows), BF16),
            pltpu.VMEM((owners, 1, LANES), jnp.int32),
            pltpu.VMEM((1, pulls), jnp.int32),
            pltpu.VMEM((owners, width, LANES), BF16),
            pltpu.VMEM((width, pulls), BF16),
            pltpu.VMEM((width, uses), BF16),
            pltpu.VMEM((width, uses), BF16),
            pltpu.VMEM((width, triples), F32),
            pltpu.VMEM((narrow, triples), F32),
            pltpu.VMEM((narrow, triples), F32),
            pltpu.VMEM((padded, triples), F32),
            pltpu.VMEM((width, pulls), BF16),
            pltpu.VMEM((width, rows), F32),
            pltpu.VMEM((width, rows), BF16),
            pltpu.VMEM((6, big, rows // 4), BF16),
            pltpu.VMEM((width, rows), BF16),
            pltpu.VMEM((units, 16, LANES), BF16),
            pltpu.VMEM((units // 2, 16, LANES), BF16),
            pltpu.VMEM((6, units // 16, 16, LANES), BF16),
            pltpu.VMEM((chips, units // 8 // chips, 16, LANES), BF16),
            pltpu.VMEM((units, 16, LANES), BF16),
            dma((2,)),
            dma((owners,)), dma((owners,)), dma((owners,)), dma((owners,)),
            dma((owners,)), dma((owners,)),
            dma((6,)), dma((6,)), dma((6,)), dma((6,)),
            dma((2,)), dma((2,)), dma((6,)), dma((6,)), dma((chips,)), dma((chips,)),
            dma((chips,)), dma((chips,)), dma((6,)), dma((6,)),
        ],
        compiler_params=pltpu.CompilerParams(
            collective_id=0, has_side_effects=True, vmem_limit_bytes=VMEM_LIMIT
        ),
        name="step",
    )(table, phase, requests, slots, relation)
    new_entity, new_entity_state = adagrad(table, entity_state, grad, 512)
    new_phase, new_phase_state = adagrad(phase, phase_state, rel_total, 1024)
    return (new_entity, new_entity_state, new_phase, new_phase_state)


def solution(mesh):
    placed = (
        P("owner", None),
        P("owner"),
        P(),
        P(),
        P(("owner", "dp"), None, None),
        P(("owner", "dp"), None),
        P(("owner", "dp"), None),
        P(("owner", "dp"), None, None),
        P(("owner", "dp"), None),
    )
    return jax.shard_map(
        on_device,
        mesh=mesh,
        in_specs=placed,
        out_specs=(P("owner", None), P("owner"), P(), P()),
        check_vma=False,
    )
```

time: 304 us -> 203 us (0.67)
  waiting for transfers between devices: 100 us -> 0 us
  between operations: 14.1 us -> 0.65 us
  Pallas kernels: 184 us -> 197 us
    psum x1 -> x0, waiting for transfers between devices: 100 us -> none  [on_device(): rel_total = lax.psum(rel_grad, ('owner', 'dp'))]
    pallas_call x2 -> x1, Pallas kernels: 170 us -> 183 us  [on_device(): pl.pallas_call(functools.partial(step_kernel, owners, triples // 2, neg),...]
  transfers between devices with their start and end apart: 1 -> 0, of which waited for: 1 -> 0; matrix products, arithmetic and copies ran while one was open for 0% -> 0% of each run, Pallas kernels for 34% -> 0%
where the time goes in v2:
time: 203 us; the launch traced here: 202 us
  Pallas kernels  197 us (97%)
  other arithmetic  2.74 us (1%)
    pallas_call x1, Pallas kernels, on_device(): pl.pallas_call(functools.partial(step_kernel, owners, triples // 2, neg),...  183 us
    pallas_call x2, Pallas kernels, adagrad(): pl.pallas_call(adagrad_kernel, grid=(pl.cdiv(rows, tile),), out_shape=(ja...  13.7 us

profile of v2, /device:TPU:1, one launch (start us, length us, event | category | flops | bytes accessed | tf_op | source)
XLA Modules:
  0.0 201.9 jit_solution(14631349864462676521)
XLA Ops:
  0.6 0.7 copy.13
  1.3 1.3 pad_add_fusion.slots
  2.6 0.0 copy-start
  2.6 183.5 %step.1 = (bf16[400,2048]{1,0:T(8,128)(2,1)}, bf16[208,7424]{1,0:T(8,128)(2,1)}) custom-call(f32[400,2048]{1,0:T(8,128)} %bitcast.11, f32[200,7424]{1,0:T(8,128)} %bitcast.9, s32[32,1,128]{2,1,0:T(1,128)} %bitcast.14, s32[1,3072]{1,0:T(1,128)} %pad_add_fusion.slots, s32[1,512]{1,0:T(1,128)} %relation.1), custom_call_target="tpu_custom_call" | custom-call | tf_op jit(solution)/shard_map/step/pallas_call | solution.py:599
  186.1 0.0 copy-done
  186.1 0.6 broadcast_in_dim.7.state
  186.8 8.8 %shard_map.121 = (f32[200,7424]{1,0:T(8,128)}, f32[1,7424]{1,0:T(1,128)}) custom-call(f32[200,7424]{1,0:T(8,128)} %bitcast.10, f32[1,7424]{1,0:T(1,128)} %broadcast_in_dim.7.state, bf16[208,7424]{1,0:T(8,128)(2,1)} %get-tuple-element.13.grad), custom_call_target="tpu_custom_call" | custom-call | tf_op jit(solution)/shard_map/pallas_call | solution.py:562
  195.6 1.4 reduce
  197.0 4.9 %shard_map.120 = (f32[400,2048]{1,0:T(8,128)}, f32[1,2048]{1,0:T(1,128)}) custom-call(f32[400,2048]{1,0:T(8,128)} %bitcast.12, f32[1,2048]{1,0:T(1,128)} %bitcast.15, bf16[400,2048]{1,0:T(8,128)(2,1)} %get-tuple-element.10.grad), custom_call_target="tpu_custom_call" | custom-call | tf_op jit(solution)/shard_map/pallas_call | solution.py:562
Async XLA Ops:
  2.6 183.5 %copy-start = (f32[7424]{0:T(1024)S(1)}, f32[7424]{0:T(1024)}, u32[]{:S(2)}) copy-start(f32[7424]{0:T(1024)} %param.12) | copy-start | bytes 89092

commit v3 on v2

--- a/solution.py
+++ b/solution.py
@@ -49,10 +49,11 @@
 
 def positions(slots, me, nx, ny):
     chip = slots >> 8
+    way = 1 - 2 * ((slots >> 7) & 1)
     x, y = chip // ny, chip & (ny - 1)
     mine = me // 2
-    dx = (mine // ny - x) & (nx - 1)
-    dy = (mine % ny - y) & (ny - 1)
+    dx = (way * (mine // ny - x)) & (nx - 1)
+    dy = (way * (mine % ny - y)) & (ny - 1)
     j = ((dy - dx) & (ny - 1)) * nx + dx
     return j * PAIR + (slots & (PAIR - 1))
 
@@ -225,7 +226,7 @@
     table, phase, table_half, asked, asked_row, sent, pulled, used, grads,
     theta, cosine, sine, phase_grads,
     received, total, shared, dp_in, full,
-    rel, core_in, ring_in, plane_in, rel_sum,
+    rel, core_in, halved, ring_in, plane_in, rel_sum,
     load_sems, ask_send, ask_recv, row_send, row_recv, back_send, back_recv,
     dp_send, dp_recv, all_send, all_recv,
     core_send, core_recv, ring_send, ring_recv, plane_send, plane_recv,
@@ -242,17 +243,30 @@
     load_phase.start()
     greet(me, owners, dp_me, 4)
 
-    def each_core(j, sign, act):
+    def owner_at(j, q):
+        return partner(me, j, nx, ny, 2 * q - 1) + q
+
+    def worker_at(j, q):
+        return partner(me, j, nx, ny, 1 - 2 * core) + q
+
+    def each_core(j, place_of, act):
         for q in range(2):
-            to = partner(me, j, nx, ny, sign) + q
+            to = place_of(j, q)
 
             @pl.when(to != me)
             def _():
                 act(q, to)
 
-    def over_chips(low, high, sign, act):
+    def over_chips(low, high, place_of, act):
         def body(j, _):
-            each_core(j, sign, functools.partial(act, j))
+            each_core(j, place_of, functools.partial(act, j))
+            return 0
+
+        lax.fori_loop(low, high, body, 0)
+
+    def loop(low, high, act):
+        def body(j, _):
+            act(j)
             return 0
 
         lax.fori_loop(low, high, body, 0)
@@ -264,7 +278,7 @@
             device_id={"owner": to}, device_id_type=MESH,
         )
 
-    over_chips(0, chips, -1, lambda j, q, to: ask(j, q, to).start())
+    over_chips(0, chips, owner_at, lambda j, q, to: ask(j, q, to).start())
     asked[core] = requests[me]
     load_table.wait()
     table_half[...] = table[...].astype(BF16)
@@ -278,7 +292,7 @@
         )
 
     def fetch(j, _):
-        each_core(j, 1, lambda q, to: arrive(asked.at[2 * j + q], ask_recv.at[2 * j + q]))
+        each_core(j, worker_at, lambda q, to: arrive(asked.at[2 * j + q], ask_recv.at[2 * j + q]))
         wanted = jnp.concatenate([asked[2 * j], asked[2 * j + 1]], 1)
         asked_row[:, lanes(j * PAIR, PAIR)] = wanted
         rows = jnp.dot(
@@ -286,7 +300,7 @@
         ).astype(BF16)
         for q in range(2):
             sent[2 * j + q] = rows[:, q * LANES : (q + 1) * LANES]
-        each_core(j, 1, lambda q, to: row_copy(j, q, to).start())
+        each_core(j, worker_at, lambda q, to: row_copy(j, q, to).start())
         return 0
 
     lax.fori_loop(0, chips, fetch, 0)
@@ -296,7 +310,7 @@
     rel_index = relation[...]
     nrel = phase.shape[1]
     width = phase.shape[0]
-    step = 512
+    step = 1024
     whole = nrel // step
 
     def phase_part(start, size):
@@ -326,7 +340,7 @@
         if low == high:
             continue
         over_chips(
-            low, high, -1,
+            low, high, owner_at,
             lambda j, q, to: arrive(
                 pulled.at[:, lanes(j * PAIR + q * LANES, LANES)], row_recv.at[2 * j + q]
             ),
@@ -369,66 +383,68 @@
     if units > tiles * per_tile:
         rel[tiles * per_tile :] = jnp.zeros_like(rel[tiles * per_tile :])
 
-    by_core, by_dp, by_chip = units // 2, units // 8, units // 8 // chips
-    core_base = core * by_core
-    dp_base = core_base + dp_me * by_dp
-    my_base = dp_base + me // 2 * by_chip
+    by_chip, by_piece = units // 2 // chips, units // 8 // chips
+    by_core = units // 2
+    my_chip = me // 2
     sibling = me + 1 - 2 * core
+    my_chip_base = core * by_core + my_chip * by_chip
+    my_piece = rel_sum.at[pl.ds(my_chip_base + dp_me * by_piece, by_piece)]
     swap = pltpu.make_async_remote_copy(
         src_ref=rel.at[pl.ds((1 - core) * by_core, by_core)], dst_ref=core_in,
         send_sem=core_send.at[0], recv_sem=core_recv.at[0],
         device_id={"owner": sibling}, device_id_type=MESH,
     )
     swap.start()
+    some = chips // 2
     ring = RingSum(
-        dp_me,
-        lambda z, h: rel.at[pl.ds(core_base + z * by_dp + h * (by_dp // 2), by_dp // 2)],
+        dp_me, lambda z, h: halved.at[pl.ds(h * some, some), z],
         [ring_in.at[i] for i in range(6)], ring_send, ring_recv,
     )
 
+    def plane_peer(j, sign):
+        return partner(me, j, nx, ny, sign * (1 - 2 * core)) + core
+
     def plane_copy(j):
-        to = partner(me, j, nx, ny, 1) + core
+        to = plane_peer(j, 1)
         return pltpu.make_async_remote_copy(
-            src_ref=rel.at[pl.ds(dp_base + to // 2 * by_chip, by_chip)], dst_ref=plane_in.at[j],
+            src_ref=halved.at[to // 2, dp_me], dst_ref=plane_in.at[j],
             send_sem=plane_send.at[j], recv_sem=plane_recv.at[j],
             device_id={"owner": to}, device_id_type=MESH,
         )
 
+    def along_dp(k):
+        return pltpu.make_async_remote_copy(
+            src_ref=my_piece, dst_ref=my_piece,
+            send_sem=gather_send.at[k - 1], recv_sem=gather_recv.at[k - 1],
+            device_id={"dp": (dp_me + k) % 4}, device_id_type=MESH,
+        )
+
     def spread_copy(j):
-        to = partner(me, j, nx, ny, 1) + core
-        mine = rel_sum.at[pl.ds(my_base, by_chip)]
+        mine = rel_sum.at[pl.ds(my_chip_base, by_chip)]
         return pltpu.make_async_remote_copy(
             src_ref=mine, dst_ref=mine,
             send_sem=spread_send.at[j], recv_sem=spread_recv.at[j],
-            device_id={"owner": to}, device_id_type=MESH,
-        )
-
-    def loop(low, high, act):
-        def body(j, _):
-            act(j)
-            return 0
-
-        lax.fori_loop(low, high, body, 0)
-
-    rel_ring = RingGather(
-        dp_me,
-        lambda z, h: rel_sum.at[pl.ds(core_base + z * by_dp + h * (by_dp // 2), by_dp // 2)],
-        gather_send, gather_recv,
-    )
-    share_core = rel_sum.at[pl.ds(core_base, by_core)]
+            device_id={"owner": plane_peer(j, 1)}, device_id_type=MESH,
+        )
+
+    share_core = rel_sum.at[pl.ds(core * by_core, by_core)]
     give = pltpu.make_async_remote_copy(
         src_ref=share_core, dst_ref=share_core,
         send_sem=core_send.at[1], recv_sem=core_recv.at[1],
         device_id={"owner": sibling}, device_id_type=MESH,
     )
 
-    over_chips(0, chips, 1, lambda j, q, to: row_copy(j, q, to).wait_send())
-
-    def back_copy(j, q, to):
+    over_chips(0, chips, worker_at, lambda j, q, to: row_copy(j, q, to).wait_send())
+    features = total.shape[0]
+    middle = -(-features // 32) * 16
+    parts = ((0, middle), (middle, features))
+
+    def back_copy(part, j, q, to):
+        low, high = parts[part]
         return pltpu.make_async_remote_copy(
-            src_ref=sent.at[2 * j + q],
-            dst_ref=received.at[:, lanes(j * PAIR + core * LANES, LANES)],
-            send_sem=back_send.at[2 * j + q], recv_sem=back_recv.at[2 * j + core],
+            src_ref=sent.at[2 * j + q, pl.ds(low, high - low)],
+            dst_ref=received.at[pl.ds(low, high - low), lanes(j * PAIR + core * LANES, LANES)],
+            send_sem=back_send.at[part, 2 * j + q], recv_sem=back_recv.at[part, 2 * j + core],
             device_id={"owner": to}, device_id_type=MESH,
         )
 
@@ -438,93 +454,126 @@
         ).astype(BF16)
         for q in range(2):
             sent[2 * j + q] = sums[:, q * LANES : (q + 1) * LANES]
-        each_core(j, -1, lambda q, to: back_copy(j, q, to).start())
+        each_core(j, owner_at, lambda q, to: back_copy(0, j, q, to).start())
         return 0
 
     first = min(4, chips)
-    later = max(first, chips - 2)
+    later = max(first, chips - 3)
     lax.fori_loop(0, first, push, 0)
     received[:, lanes(core * LANES, LANES)] = sent[core]
     arrive(core_in, core_recv.at[0])
-    own_core = rel.at[pl.ds(core_base, by_core)]
-    own_core[...] = (own_core[...].astype(F32) + core_in[...].astype(F32)).astype(BF16)
+
+    def add_core(p):
+        own = rel[pl.ds(core * by_core + p * by_chip, by_chip)].astype(F32)
+        both = own + core_in[pl.ds(p * by_chip, by_chip)].astype(F32)
+        halved[p] = both.astype(BF16).reshape(4, by_piece, 16, LANES)
+
+    loop(0, chips, add_core)
     ring.begin()
     lax.fori_loop(first, later, push, 0)
     ring.relay()
     lax.fori_loop(later, chips, push, 0)
+    over_chips(0, chips, owner_at, lambda j, q, to: back_copy(1, j, q, to).start())
     for h in range(2):
         spot = ring.piece(dp_me, h)
         spot[...] = (spot[...].astype(F32) + ring.finish(h)).astype(BF16)
     loop(1, chips, lambda j: plane_copy(j).start())
 
-    half = chips // 2 if chips > 1 else chips
     rows = total.shape[1]
-
-    def scatter(low, high):
+    share = rows // 4
+
+    def scatter(part):
+        low, high = parts[part]
         over_chips(
-            low, high, 1,
+            0, chips, worker_at,
             lambda j, q, to: arrive(
-                received.at[:, lanes(j * PAIR + q * LANES, LANES)], back_recv.at[2 * j + q]
+                received.at[pl.ds(low, high - low), lanes(j * PAIR + q * LANES, LANES)],
+                back_recv.at[part, 2 * j + q],
             ),
         )
-        span = slice(low * PAIR, high * PAIR)
         for t in range(rows // tile):
             cols = slice(t * tile, (t + 1) * tile)
             added = lax.dot_general(
-                received[:, span], one_hot(tile, t * tile, asked_row[:, span]), NT,
+                received[low:high], one_hot(tile, t * tile, asked_row[...]), NT,
                 preferred_element_type=F32,
             )
-            if low == 0:
-                total[:, cols] = added
-            else:
-                total[:, cols] += added
-
-    scatter(0, half)
-    mine = rel.at[pl.ds(my_base, by_chip)][...].astype(F32)
+            total[low:high, cols] = added
+            shared[low:high, cols] = added.astype(BF16)
+
+    def halves(part):
+        low, high = parts[part]
+        cut = low + -(-(high - low) // 32) * 16
+        return ((low, cut - low), (cut, high - cut))
+
+    def piece_of(ref, part):
+        return lambda z, h: ref.at[pl.ds(*halves(part)[h]), lanes(z * share, share)]
+
+    def dp_sum(part):
+        sizes = [halves(part)[h][1] for h in (0, 1, 1, 0, 0, 1)]
+        return RingSum(
+            dp_me, piece_of(shared, part),
+            [dp_in.at[part, i, pl.ds(0, sizes[i])] for i in range(6)],
+            dp_send.at[part], dp_recv.at[part],
+        )
+
+    sums = [dp_sum(part) for part in range(2)]
+    alls = [
+        RingGather(dp_me, piece_of(full, part), all_send.at[part], all_recv.at[part])
+        for part in range(2)
+    ]
+
+    def settle(part):
+        for h in range(2):
+            own = piece_of(total, part)(dp_me, h)
+            alls[part].piece(dp_me, h)[...] = (own[...] + sums[part].finish(h)).astype(BF16)
+        alls[part].begin()
+
+    scatter(0)
+    sums[0].begin()
 
     def add_plane(j, value):
         arrive(plane_in.at[j], plane_recv.at[j])
         return value + plane_in[j].astype(F32)
 
-    rel_sum[pl.ds(my_base, by_chip)] = lax.fori_loop(1, chips, add_plane, mine).astype(BF16)
+    my_piece[...] = lax.fori_loop(
+        1, chips, add_plane, halved[my_chip, dp_me].astype(F32)
+    ).astype(BF16)
+    for k in range(1, 4):
+        along_dp(k).start()
+    sums[0].relay()
+    scatter(1)
+    sums[1].begin()
+    for k in range(1, 4):
+        z = (dp_me - k + 4) % 4
+        arrive(
+            rel_sum.at[pl.ds(my_chip_base + z * by_piece, by_piece)], gather_recv.at[k - 1]
+        )
     loop(1, chips, lambda j: spread_copy(j).start())
+    settle(0)
+    sums[1].relay()
+    alls[0].relay()
+    settle(1)
+    alls[1].relay()
 
     def spread_in(j):
-        chip = partner(me, j, nx, ny, -1) // 2
-        arrive(rel_sum.at[pl.ds(dp_base + chip * by_chip, by_chip)], spread_recv.at[j])
+        chip = plane_peer(j, -1) // 2
+        arrive(rel_sum.at[pl.ds(core * by_core + chip * by_chip, by_chip)], spread_recv.at[j])
 
     loop(1, chips, spread_in)
-    rel_ring.begin()
-    if half < chips:
-        scatter(half, chips)
-
-    share = rows // 4
-    split = total.shape[0] // 32 * 16
-    shared[...] = total[...].astype(BF16)
-
-    def piece_of(ref):
-        def piece(z, h):
-            features = pl.ds(0, split) if h == 0 else pl.ds(split, ref.shape[0] - split)
-            return ref.at[features, lanes(z * share, share)]
-
-        return piece
-
-    big = shared.shape[0] - split
-    dp_ring = RingSum(
-        dp_me, piece_of(shared),
-        [dp_in.at[i, pl.ds(0, big if i in (1, 2, 5) else split)] for i in range(6)],
-        dp_send, dp_recv,
-    )
-    dp_ring.begin()
-    rel_ring.relay()
-    dp_ring.relay()
-    rel_ring.finish()
     give.start()
-    all_ring = RingGather(dp_me, piece_of(full), all_send, all_recv)
-    for h in range(2):
-        own = total.at[pl.ds(0, split) if h == 0 else pl.ds(split, big), lanes(dp_me * share, share)]
-        all_ring.piece(dp_me, h)[...] = (own[...] + dp_ring.finish(h)).astype(BF16)
-    all_ring.begin()
+    swap.wait_send()
+    ring.drain()
+    for part in range(2):
+        sums[part].drain()
+    for k in range(1, 4):
+        along_dp(k).wait_send()
+    loop(1, chips, lambda j: plane_copy(j).wait_send())
+    loop(1, chips, lambda j: spread_copy(j).wait_send())
+    over_chips(0, chips, owner_at, lambda j, q, to: ask(j, q, to).wait_send())
+    for part in range(2):
+        over_chips(
+            0, chips, owner_at, lambda j, q, to: back_copy(part, j, q, to).wait_send()
+        )
     arrive(rel_sum.at[pl.ds((1 - core) * by_core, by_core)], core_recv.at[1])
 
     def lay(t):
@@ -533,19 +582,12 @@
         )
 
     loop(0, tiles, lay)
-    all_ring.relay()
-    swap.wait_send()
     give.wait_send()
-    ring.drain()
-    rel_ring.drain()
-    dp_ring.drain()
-    loop(1, chips, lambda j: plane_copy(j).wait_send())
-    loop(1, chips, lambda j: spread_copy(j).wait_send())
-    over_chips(0, chips, -1, lambda j, q, to: ask(j, q, to).wait_send())
-    over_chips(0, chips, -1, lambda j, q, to: back_copy(j, q, to).wait_send())
-    all_ring.finish()
+    for part in range(2):
+        alls[part].finish()
     grad_out[...] = full[...]
-    all_ring.drain()
+    for part in range(2):
+        alls[part].drain()
 
 
 def adagrad_kernel(table, state, grad, new_table, new_state):
@@ -594,8 +636,9 @@
     dma = pltpu.SemaphoreType.DMA
     chips = owners // 2
     padded = -(-narrow // 16) * 16
-    units = -(-nrel // LANES * padded // 16 // (16 * chips)) * 16 * chips
-    big = width - width // 32 * 16
+    units = -(-(nrel // LANES * padded // 16) // (8 * chips)) * 8 * chips
+    biggest = -(-width // 64) * 16
+    piece = units // 8 // chips
     grad, rel_total = pl.pallas_call(
         functools.partial(step_kernel, owners, triples // 2, neg),
         out_shape=(
@@ -621,19 +664,20 @@
             pltpu.VMEM((width, pulls), BF16),
             pltpu.VMEM((width, rows), F32),
             pltpu.VMEM((width, rows), BF16),
-            pltpu.VMEM((6, big, rows // 4), BF16),
+            pltpu.VMEM((2, 6, biggest, rows // 4), BF16),
             pltpu.VMEM((width, rows), BF16),
             pltpu.VMEM((units, 16, LANES), BF16),
             pltpu.VMEM((units // 2, 16, LANES), BF16),
-            pltpu.VMEM((6, units // 16, 16, LANES), BF16),
-            pltpu.VMEM((chips, units // 8 // chips, 16, LANES), BF16),
+            pltpu.VMEM((chips, 4, piece, 16, LANES), BF16),
+            pltpu.VMEM((6, chips // 2, piece, 16, LANES), BF16),
+            pltpu.VMEM((chips, piece, 16, LANES), BF16),
             pltpu.VMEM((units, 16, LANES), BF16),
             dma((2,)),
             dma((owners,)), dma((owners,)), dma((owners,)), dma((owners,)),
-            dma((owners,)), dma((owners,)),
-            dma((6,)), dma((6,)), dma((6,)), dma((6,)),
+            dma((2, owners)), dma((2, owners)),
+            dma((2, 6)), dma((2, 6)), dma((2, 6)), dma((2, 6)),
             dma((2,)), dma((2,)), dma((6,)), dma((6,)), dma((chips,)), dma((chips,)),
-            dma((chips,)), dma((chips,)), dma((6,)), dma((6,)),
+            dma((chips,)), dma((chips,)), dma((3,)), dma((3,)),
         ],
         compiler_params=pltpu.CompilerParams(
             collective_id=0, has_side_effects=True, vmem_limit_bytes=VMEM_LIMIT

time: 203 us -> 166 us (0.82)
  Pallas kernels: 197 us -> 161 us
    pallas_call x1, Pallas kernels: 183 us -> 147 us  [on_device(): pl.pallas_call(functools.partial(step_kernel, owners, triples // 2, neg),...]
where the time goes in v3:
time: 166 us
  Pallas kernels  161 us (97%)
  other arithmetic  2.74 us (2%)
    pallas_call x1, Pallas kernels, on_device(): pl.pallas_call(functools.partial(step_kernel, owners, triples // 2, neg),...  147 us
    pallas_call x2, Pallas kernels, adagrad(): pl.pallas_call(adagrad_kernel, grid=(pl.cdiv(rows, tile),), out_shape=(ja...  13.7 us

profile of v3, /device:TPU:1, one launch (start us, length us, event | category | flops | bytes accessed | tf_op | source)
XLA Modules:
  0.0 165.5 jit_solution(14092321949038027201)
XLA Ops:
  0.6 0.7 copy.13
  1.3 1.3 pad_add_fusion.slots
  2.6 0.0 copy-start
  2.6 147.1 %step.1 = (bf16[400,2048]{1,0:T(8,128)(2,1)}, bf16[208,7424]{1,0:T(8,128)(2,1)}) custom-call(f32[400,2048]{1,0:T(8,128)} %bitcast.11, f32[200,7424]{1,0:T(8,128)} %bitcast.9, s32[32,1,128]{2,1,0:T(1,128)} %bitcast.14, s32[1,3072]{1,0:T(1,128)} %pad_add_fusion.slots, s32[1,512]{1,0:T(1,128)} %relation.1), custom_call_target="tpu_custom_call" | custom-call | tf_op jit(solution)/shard_map/step/pallas_call | solution.py:642
  149.7 0.0 copy-done
  149.7 0.6 broadcast_in_dim.7.state
  150.3 8.8 %shard_map.121 = (f32[200,7424]{1,0:T(8,128)}, f32[1,7424]{1,0:T(1,128)}) custom-call(f32[200,7424]{1,0:T(8,128)} %bitcast.10, f32[1,7424]{1,0:T(1,128)} %broadcast_in_dim.7.state, bf16[208,7424]{1,0:T(8,128)(2,1)} %get-tuple-element.13.grad), custom_call_target="tpu_custom_call" | custom-call | tf_op jit(solution)/shard_map/pallas_call | solution.py:604
  159.2 1.4 reduce
  160.6 4.9 %shard_map.120 = (f32[400,2048]{1,0:T(8,128)}, f32[1,2048]{1,0:T(1,128)}) custom-call(f32[400,2048]{1,0:T(8,128)} %bitcast.12, f32[1,2048]{1,0:T(1,128)} %bitcast.15, bf16[400,2048]{1,0:T(8,128)(2,1)} %get-tuple-element.10.grad), custom_call_target="tpu_custom_call" | custom-call | tf_op jit(solution)/shard_map/pallas_call | solution.py:604
Async XLA Ops:
  2.6 147.1 %copy-start = (f32[7424]{0:T(1024)S(1)}, f32[7424]{0:T(1024)}, u32[]{:S(2)}) copy-start(f32[7424]{0:T(1024)} %param.12) | copy-start | bytes 89092

commit v4 on v3

v4 whole, which is shorter than its diff:
```python
import functools

import jax
import jax.numpy as jnp
from jax import lax
from jax.experimental import pallas as pl
from jax.experimental.pallas import tpu as pltpu
from jax.sharding import PartitionSpec as P

GAMMA = 2.0
RATE = 0.05
LANES = 128
PAIR = 256
BF16 = jnp.bfloat16
F32 = jnp.float32
MESH = pl.DeviceIdType.MESH
VMEM_LIMIT = 60 * 2**20
NT = (((1,), (1,)), ((), ()))
TN = (((0,), (0,)), ((), ()))


def one_hot(rows, base, index):
    at = lax.broadcasted_iota(jnp.int32, (rows, index.shape[1]), 0) + base
    return jnp.where(at == index, 1.0, 0.0).astype(BF16)


def lanes(start, size):
    return pl.ds(pl.multiple_of(start, LANES), size)


def grid_of(owners):
    chips = owners // 2
    along_y = min(4, chips)
    return chips // along_y, along_y


def partner(me, j, nx, ny, back):
    chip = lax.div(me, 2)
    x, y = lax.div(chip, ny), lax.rem(chip, ny)
    if isinstance(j, int):
        dx = j % nx
        dy = (j // nx + dx) % ny
    else:
        dx = lax.rem(j, nx)
        dy = lax.rem(lax.div(j, nx) + dx, ny)
    x = lax.rem(x + (1 - 2 * back) * dx + back * nx, nx)
    y = lax.rem(y + (1 - 2 * back) * dy + back * ny, ny)
    return (x * ny + y) * 2


def positions(slots, me, nx, ny):
    chip = slots >> 8
    way = 1 - 2 * ((slots >> 7) & 1)
    x, y = chip // ny, chip & (ny - 1)
    mine = me // 2
    dx = (way * (mine // ny - x)) & (nx - 1)
    dy = (way * (mine % ny - y)) & (ny - 1)
    j = ((dy - dx) & (ny - 1)) * nx + dx
    return j * PAIR + (slots & (PAIR - 1))


def as_column(row):
    return jnp.broadcast_to(row, (LANES, row.shape[1])).T[:, :1]


def as_row(column):
    return jnp.broadcast_to(column, (column.shape[0], LANES)).T[:1, :]


def greet(me, owners, dp_me, dps):
    barrier = pltpu.get_barrier_semaphore()

    def hello(k, _):
        pl.semaphore_signal(
            barrier, inc=1, device_id={"owner": (me + k) % owners}, device_id_type=MESH
        )
        return 0

    lax.fori_loop(1, owners, hello, 0)
    for k in range(1, dps):
        pl.semaphore_signal(
            barrier, inc=1, device_id={"dp": (dp_me + k) % dps}, device_id_type=MESH
        )
    pl.semaphore_wait(barrier, owners - 1 + dps - 1)


def block_grads(b, group, neg, used, cosine, sine, grads, phase_grads):
    triples = 2 * group
    cols = lanes(b * group, group)
    tail_cols = lanes(triples + b * group, group)
    neg_cols = lanes(2 * triples + b * neg, neg)
    cos, sin = cosine[:, cols], sine[:, cols]
    width = cos.shape[0]
    heads = used[:, cols].astype(F32)
    head_re, head_im = heads[:width], heads[width:]
    rot_re = head_re * cos - head_im * sin
    rot_im = head_re * sin + head_im * cos
    rotated = jnp.concatenate([rot_re, rot_im], 0)
    diff = rotated - used[:, tail_cols].astype(F32)
    pos_score = GAMMA - jnp.sum(diff * diff, 0, keepdims=True)
    rot_half = rotated.astype(BF16)
    rot_wide = rot_half.astype(F32)
    negs = used[:, neg_cols]
    neg_wide = negs.astype(F32)
    row_norm = as_column(jnp.sum(rot_wide * rot_wide, 0, keepdims=True))
    neg_norm = jnp.sum(neg_wide * neg_wide, 0, keepdims=True)
    cross = lax.dot_general(rot_half, negs, TN, preferred_element_type=F32)
    neg_score = GAMMA - (row_norm + neg_norm - 2.0 * cross)
    weight = jax.nn.sigmoid(neg_score) * (1.0 / neg)
    weight_half = weight.astype(BF16)
    diff_grad = (2.0 * jax.nn.sigmoid(-pos_score)) * diff
    row_sum = as_row(jnp.sum(weight, 1, keepdims=True))
    col_sum = jnp.sum(weight, 0, keepdims=True)
    rot_grad = (
        diff_grad
        - (2.0 * row_sum) * rot_wide
        + 2.0 * lax.dot_general(negs, weight_half, NT, preferred_element_type=F32)
    )
    grads[:, neg_cols] = (
        2.0 * jnp.dot(rot_half, weight_half, preferred_element_type=F32)
        - (2.0 * col_sum) * neg_wide
    ).astype(BF16)
    grads[:, tail_cols] = (-diff_grad).astype(BF16)
    grad_re, grad_im = rot_grad[:width], rot_grad[width:]
    phase_grads[:width, cols] = grad_im * rot_re - grad_re * rot_im
    grads[:, cols] = jnp.concatenate(
        [grad_re * cos + grad_im * sin, grad_im * cos - grad_re * sin], 0
    ).astype(BF16)


def arrive(ref, sem):
    pltpu.make_async_copy(ref, ref, sem).wait()


class RingSum:
    def __init__(self, dp_me, piece, landing, send, recv):
        self.piece, self.landing, self.send, self.recv = piece, landing, send, recv
        self.me, self.right, self.left = dp_me, (dp_me + 1) % 4, (dp_me + 3) % 4
        self.opposite = (dp_me + 2) % 4

    def copy(self, src, slot, to):
        return pltpu.make_async_remote_copy(
            src_ref=src, dst_ref=self.landing[slot],
            send_sem=self.send.at[slot], recv_sem=self.recv.at[slot],
            device_id={"dp": to}, device_id_type=MESH,
        )

    def part(self, slot):
        z, h, to = (
            (self.opposite, 0, self.right),
            (self.opposite, 1, self.left),
            (self.right, 1, self.right),
            (self.left, 0, self.left),
            (self.right, 0, self.right),
            (self.left, 1, self.left),
        )[slot]
        return self.copy(self.piece(z, h), slot, to)

    def begin(self):
        for slot in range(4):
            self.part(slot).start()

    def relay(self):
        for slot, z, h in ((0, self.right, 0), (1, self.left, 1)):
            arrive(self.landing[slot], self.recv.at[slot])
            spot = self.piece(z, h)
            spot[...] = (spot[...].astype(F32) + self.landing[slot][...].astype(F32)).astype(BF16)
            self.part(4 + slot).start()

    def finish(self, h):
        slots = (4, 3) if h == 0 else (5, 2)
        for slot in slots:
            arrive(self.landing[slot], self.recv.at[slot])
        return self.landing[slots[0]][...].astype(F32) + self.landing[slots[1]][...].astype(F32)

    def drain(self):
        for slot in range(6):
            self.part(slot).wait_send()


class RingGather:
    def __init__(self, me, count, device, piece, send, recv):
        self.device, self.piece, self.send, self.recv = device, piece, send, recv
        self.count = count
        self.me, self.right, self.left = me, (me + 1) % count, (me + count - 1) % count
        self.opposite = (me + 2) % count

    def part(self, slot):
        z, h, to = (
            (self.me, 0, self.right),
            (self.me, 1, self.left),
            (self.me, 1, self.right),
            (self.me, 0, self.left),
            (self.left, 0, self.right),
            (self.right, 1, self.left),
        )[slot]
        return pltpu.make_async_remote_copy(
            src_ref=self.piece(z, h), dst_ref=self.piece(z, h),
            send_sem=self.send.at[slot], recv_sem=self.recv.at[slot],
            device_id=self.device(to), device_id_type=MESH,
        )

    def begin(self):
        if self.count == 4:
            for slot in range(4):
                self.part(slot).start()

    def relay(self):
        if self.count == 4:
            arrive(self.piece(self.left, 0), self.recv.at[0])
            self.part(4).start()
            arrive(self.piece(self.right, 1), self.recv.at[1])
            self.part(5).start()

    def finish(self):
        if self.count == 4:
            arrive(self.piece(self.left, 1), self.recv.at[2])
            arrive(self.piece(self.right, 0), self.recv.at[3])
            arrive(self.piece(self.opposite, 0), self.recv.at[4])
            arrive(self.piece(self.opposite, 1), self.recv.at[5])

    def drain(self):
        if self.count == 4:
            for slot in range(6):
                self.part(slot).wait_send()


class DirectGather:
    def __init__(self, me, count, device, piece, send, recv):
        self.me, self.count, self.device, self.piece = me, count, device, piece
        self.send, self.recv = send, recv

    def part(self, k):
        return pltpu.make_async_remote_copy(
            src_ref=self.piece(self.me), dst_ref=self.piece(self.me),
            send_sem=self.send.at[k - 1], recv_sem=self.recv.at[k - 1],
            device_id=self.device((self.me + k) % self.count), device_id_type=MESH,
        )

    def begin(self):
        for k in range(1, self.count):
            self.part(k).start()

    def finish(self):
        for k in range(1, self.count):
            source = (self.me + self.count - k) % self.count
            arrive(self.piece(source), self.recv.at[k - 1])

    def drain(self):
        for k in range(1, self.count):
            self.part(k).wait_send()


def cut_parts(features):
    units = features // 16
    counts = (10, 9, 6) if units == 25 else (units - 4, 2, 2)
    bounds = [0]
    for count in counts:
        bounds.append(bounds[-1] + 16 * count)
    return tuple(zip(bounds[:-1], bounds[1:]))


def split_part(low, high):
    cut = low + -(-(high - low) // 32) * 16
    return ((low, cut - low), (cut, high - cut))


def step_kernel(
    owners, group, neg,
    table_hbm, phase_hbm, requests, slots, relation,
    grad_out, rel_out,
    table, phase, table_half, asked, asked_column, sent, pulled, used, grads,
    theta, cosine, sine, phase_grads,
    received, total, shared, dp_in, full,
    raw, relations, share_sum, plane_in, rel_sum,
    load_sems, ask_send, ask_recv, row_send, row_recv, back_send, back_recv,
    dp_send, dp_recv, all_send, all_recv,
    core_send, core_recv, index_send, index_recv, raw_send, raw_recv,
    plane_send, plane_recv, piece_send, piece_recv,
    line_send, line_recv, sheet_send, sheet_recv,
):
    nx, ny = grid_of(owners)
    chips = nx * ny
    me = lax.axis_index("owner")
    dp_me = lax.axis_index("dp")
    core = me % 2
    load_table = pltpu.make_async_copy(table_hbm, table, load_sems.at[0])
    load_phase = pltpu.make_async_copy(phase_hbm, phase, load_sems.at[1])
    load_table.start()
    load_phase.start()
    greet(me, owners, dp_me, 4)

    def owner_at(j, q):
        return partner(me, j, nx, ny, 1 - q) + q

    def worker_at(j, q):
        return partner(me, j, nx, ny, core) + q

    def each_core(j, place_of, start, start_own):
        for q in range(2):
            to = place_of(j, q)
            if isinstance(j, int) and j == 0:
                pl.when(to != me)(functools.partial(start, j, q, to))
                pl.when(to == me)(functools.partial(start_own, q))
            else:
                start(j, q, to)

    def sent_all(ref, sem):
        arrive(ref.at[pl.ds(0, owners - 1)], sem)

    def loop(low, high, act):
        def body(j, _):
            act(j)
            return 0

        lax.fori_loop(low, high, body, 0)

    def ask(j, q, to):
        pltpu.make_async_remote_copy(
            src_ref=requests.at[to], dst_ref=asked.at[2 * j + core],
            send_sem=ask_send, recv_sem=ask_recv,
            device_id={"owner": to}, device_id_type=MESH,
        ).start()

    def ask_own(q):
        pltpu.make_async_copy(requests.at[me], asked.at[q], ask_recv).start()

    for j in range(chips):
        each_core(j, owner_at, ask, ask_own)

    def at_dp(z):
        return {"dp": z}

    relations[core, dp_me] = relation[...]
    indices = DirectGather(
        dp_me, 4, at_dp, lambda z: relations.at[core, z], index_send, index_recv
    )
    indices.begin()
    load_table.wait()
    table_half[...] = table[...].astype(BF16)

    cuts = (0, chips // 2, chips - chips // 4, chips)

    def row_copy(cut, j, q, to):
        pltpu.make_async_remote_copy(
            src_ref=sent.at[2 * j + q],
            dst_ref=pulled.at[:, lanes(j * PAIR + core * LANES, LANES)],
            send_sem=row_send, recv_sem=row_recv.at[cut],
            device_id={"owner": to}, device_id_type=MESH,
        ).start()

    def row_own(q):
        pltpu.make_async_copy(
            sent.at[q], pulled.at[:, q * LANES : (q + 1) * LANES], row_recv.at[0]
        ).start()

    def fetch(cut, j):
        wanted = jnp.concatenate([asked[2 * j], asked[2 * j + 1]], 1)
        asked_column[pl.ds(pl.multiple_of(j * PAIR, PAIR), PAIR)] = jnp.broadcast_to(
            wanted, (LANES, PAIR)
        ).T
        rows = jnp.dot(
            table_half[...], one_hot(table_half.shape[1], 0, wanted), preferred_element_type=F32
        ).astype(BF16)
        for q in range(2):
            sent[2 * j + q] = rows[:, q * LANES : (q + 1) * LANES]
        each_core(j, worker_at, functools.partial(row_copy, cut), row_own)

    arrive(asked, ask_recv)
    fetch(0, 0)
    for cut in range(3):
        loop(max(1, cuts[cut]), cuts[cut + 1], functools.partial(fetch, cut))

    load_phase.wait()
    rel_index = relation[...]
    nrel = phase.shape[1]
    width = phase.shape[0]
    step = 1024
    whole = nrel // step

    def phase_part(start, size):
        part = phase[:, lanes(start, size)]
        high = part.astype(BF16).astype(F32)
        both = jnp.concatenate([high, part - high], 0).astype(BF16)
        return jnp.dot(both, one_hot(size, start, rel_index), preferred_element_type=F32)

    theta[...] = jnp.zeros_like(theta)

    def add_phase(k, _):
        theta[...] += phase_part(k * step, step)
        return 0

    lax.fori_loop(0, whole, add_phase, 0)
    if nrel % step:
        theta[...] += phase_part(whole * step, nrel % step)
    angle = theta[:width] + theta[width:]
    cosine[...] = jnp.cos(angle)
    sine[...] = jnp.sin(angle)

    place = positions(slots[...], me, nx, ny)
    uses = slots.shape[1]
    tile = 256
    for cut in range(3):
        low, high = cuts[cut], cuts[cut + 1]
        if low == high:
            continue
        arrive(pulled.at[:, low * PAIR : high * PAIR], row_recv.at[cut])
        for t in range(uses // tile):
            cols = slice(t * tile, (t + 1) * tile)
            found = jnp.dot(
                pulled[:, low * PAIR : high * PAIR],
                one_hot((high - low) * PAIR, low * PAIR, place[:, cols]),
                preferred_element_type=F32,
            ).astype(BF16)
            used[:, cols] = found if low == 0 else used[:, cols] + found

    phase_grads[width:] = jnp.zeros_like(phase_grads[width:])
    for b in range(2):
        block_grads(b, group, neg, used, cosine, sine, grads, phase_grads)

    raw[core, dp_me] = phase_grads[...].astype(BF16)
    padded = raw.shape[2]
    raw_halves = split_part(0, padded)
    raw_ring = RingGather(
        dp_me, 4, at_dp, lambda z, h: raw.at[core, z, pl.ds(*raw_halves[h])],
        raw_send, raw_recv,
    )
    raw_ring.begin()
    sibling = me + 1 - 2 * core

    def to_sibling(ref, slot):
        return pltpu.make_async_remote_copy(
            src_ref=ref.at[core], dst_ref=ref.at[core],
            send_sem=core_send.at[slot], recv_sem=core_recv.at[slot],
            device_id={"owner": sibling}, device_id_type=MESH,
        )

    per_tile = padded // 16
    share_tiles = -(-(nrel // LANES) // 16) * 2
    by_piece = rel_sum.shape[4]
    chip = me // 2
    my_x, my_y = chip // ny, chip % ny
    eighth = core * 4 + dp_me

    def sum_share():
        base = eighth * share_tiles * LANES
        for t in range(share_tiles // 2):
            found = None
            for c in range(2):
                for z in range(4):
                    part = lax.dot_general(
                        raw[c, z], one_hot(PAIR, base + t * PAIR, relations[c, z]), NT,
                        preferred_element_type=F32,
                    )
                    found = part if found is None else found + part
            found = found.astype(BF16)
            for i in range(2):
                at = (2 * t + i) * per_tile
                share_sum[at : at + per_tile] = found[
                    :, i * LANES : (i + 1) * LANES
                ].reshape(per_tile, 16, LANES)
        filled = share_tiles * per_tile
        if filled < share_sum.shape[0]:
            share_sum[filled:] = jnp.zeros_like(share_sum[filled:])

    def plane_copy(j):
        to = partner(me, j, nx, ny, core)
        pltpu.make_async_remote_copy(
            src_ref=share_sum.at[pl.ds(lax.div(to, 2) * by_piece, by_piece)],
            dst_ref=plane_in.at[j], send_sem=plane_send, recv_sem=plane_recv,
            device_id={"owner": to + core}, device_id_type=MESH,
        ).start()

    def add_plane(j, value):
        return value + plane_in[j].astype(F32)

    pieces = DirectGather(
        dp_me, 4, at_dp, lambda z: rel_sum.at[core, my_x, my_y, z], piece_send, piece_recv
    )

    def at_x(x):
        return {"owner": (x * ny + my_y) * 2 + core}

    def at_y(y):
        return {"owner": (my_x * ny + y) * 2 + core}

    low_z, high_z = pl.ds(0, 2), pl.ds(2, 2)
    lines = (
        DirectGather(
            my_x, nx, at_x, lambda x: rel_sum.at[core, x, my_y, low_z],
            line_send.at[0], line_recv.at[0],
        ),
        DirectGather(
            my_y, ny, at_y, lambda y: rel_sum.at[core, my_x, y, high_z],
            line_send.at[1], line_recv.at[1],
        ),
    )

    def two(h):
        return pl.ds(2 * h, 2)

    sheets = (
        RingGather(
            my_y, ny, at_y,
            lambda y, h: rel_sum.at[core, two(h) if nx == 4 else slice(None), y,
                                    low_z if nx == 4 else pl.ds(h, 1)],
            sheet_send.at[0], sheet_recv.at[0],
        ),
        RingGather(
            my_x, nx, at_x, lambda x, h: rel_sum.at[core, x, two(h), high_z],
            sheet_send.at[1], sheet_recv.at[1],
        ),
    )

    sent_all(sent, row_send)
    parts = cut_parts(total.shape[0])
    numbers = range(len(parts))

    def back_copy(part, j, q, to):
        low, high = parts[part]
        pltpu.make_async_remote_copy(
            src_ref=sent.at[2 * j + q, pl.ds(low, high - low)],
            dst_ref=received.at[pl.ds(low, high - low), lanes(j * PAIR + core * LANES, LANES)],
            send_sem=back_send.at[part], recv_sem=back_recv.at[part],
            device_id={"owner": to}, device_id_type=MESH,
        ).start()

    def back_own(part, q):
        low, high = parts[part]
        pltpu.make_async_copy(
            sent.at[q, pl.ds(low, high - low)],
            received.at[pl.ds(low, high - low), q * LANES : (q + 1) * LANES],
            back_recv.at[part],
        ).start()

    def push(j):
        sums = lax.dot_general(
            grads[...], one_hot(PAIR, j * PAIR, place), NT, preferred_element_type=F32
        ).astype(BF16)
        for q in range(2):
            sent[2 * j + q] = sums[:, q * LANES : (q + 1) * LANES]
        send_back(0, j)

    def send_back(part, j):
        each_core(
            j, owner_at, functools.partial(back_copy, part), functools.partial(back_own, part)
        )

    def send_later(part):
        for j in range(chips):
            send_back(part, j)

    first, second, third = min(3, chips), min(7, chips), min(10, chips)
    push(0)
    loop(1, first, push)
    indices.finish()
    raw_ring.relay()
    loop(first, second, push)
    raw_ring.finish()
    to_sibling(raw, 0).start()
    to_sibling(relations, 1).start()
    loop(second, third, push)
    loop(third, chips, push)
    send_later(1)
    arrive(raw.at[1 - core], core_recv.at[0])
    arrive(relations.at[1 - core], core_recv.at[1])
    sum_share()
    for j in range(1, chips):
        plane_copy(j)

    rows = total.shape[1]
    share = rows // 4

    def scatter(part, between):
        low, high = parts[part]
        count = rows // tile
        arrive(received.at[low:high], back_recv.at[part])
        for t in range(count):
            for at, act in between:
                if at * count // 8 == t:
                    act()
            cols = slice(t * tile, (t + 1) * tile)
            row = lax.broadcasted_iota(jnp.int32, (received.shape[1], tile), 1) + t * tile
            wanted = jnp.concatenate([asked_column[...]] * (tile // LANES), 1)
            added = jnp.dot(
                received[low:high], jnp.where(wanted == row, 1.0, 0.0).astype(BF16),
                preferred_element_type=F32,
            )
            total[low:high, cols] = added
            shared[low:high, cols] = added.astype(BF16)

    def halves(part):
        return split_part(*parts[part])

    def piece_of(ref, part):
        return lambda z, h: ref.at[pl.ds(*halves(part)[h]), lanes(z * share, share)]

    def dp_sum(part):
        sizes = [halves(part)[h][1] for h in (0, 1, 1, 0, 0, 1)]
        return RingSum(
            dp_me, piece_of(shared, part),
            [dp_in.at[part, i, pl.ds(0, sizes[i])] for i in range(6)],
            dp_send.at[part], dp_recv.at[part],
        )

    sums = [dp_sum(part) for part in numbers]
    alls = [
        RingGather(
            dp_me, 4, at_dp, piece_of(full, part), all_send.at[part], all_recv.at[part]
        )
        for part in numbers
    ]

    def settle(part):
        for h in range(2):
            own = piece_of(total, part)(dp_me, h)
            alls[part].piece(dp_me, h)[...] = (own[...] + sums[part].finish(h)).astype(BF16)
        alls[part].begin()

    def sum_plane():
        mine = share_sum.at[pl.ds(chip * by_piece, by_piece)]
        arrive(plane_in.at[1:], plane_recv)
        rel_sum[core, my_x, my_y, dp_me] = lax.fori_loop(
            1, chips, add_plane, mine[...].astype(F32)
        ).astype(BF16)
        pieces.begin()

    def start_lines():
        pieces.finish()
        for line in lines:
            line.begin()

    def start_sheets():
        for line in lines:
            line.finish()
        for ring in sheets:
            ring.begin()

    def relay_sheets():
        for ring in sheets:
            ring.relay()

    def start_core():
        for ring in sheets:
            ring.finish()
        to_sibling(rel_sum, 2).start()

    scatter(0, [(6, functools.partial(send_later, 2)), (7, sum_plane)])
    sums[0].begin()
    start_lines()
    scatter(1, [(2, sums[0].relay), (4, start_sheets)])
    sums[1].begin()
    scatter(2, [
        (0, functools.partial(settle, 0)), (1, relay_sheets), (4, sums[1].relay),
        (5, alls[0].relay), (7, start_core),
    ])
    sums[2].begin()
    last = 2

    def lay(c, z):
        for unit in range(share_tiles * per_tile):
            p, i = unit // by_piece, unit % by_piece
            t, r = unit // per_tile, unit % per_tile
            cols = lanes(((c * 4 + z) * share_tiles + t) * LANES, LANES)
            rel_out[16 * r : 16 * r + 16, cols] = rel_sum[c, p // ny, p % ny, z, i]

    settle(1)
    sums[last].relay()
    loop(0, 4, lambda z: lay(core, z))
    alls[1].relay()
    settle(last)
    arrive(rel_sum.at[1 - core], core_recv.at[2])
    loop(0, 4, lambda z: lay(1 - core, z))
    alls[last].relay()

    indices.drain()
    raw_ring.drain()
    to_sibling(raw, 0).wait_send()
    to_sibling(relations, 1).wait_send()
    to_sibling(rel_sum, 2).wait_send()
    pieces.drain()
    for gather in lines + sheets:
        gather.drain()
    for part in numbers:
        sums[part].drain()
    arrive(plane_in.at[1:], plane_send)
    sent_all(asked, ask_send)
    for part, (low, high) in enumerate(parts):
        sent_all(sent.at[:, low:high], back_send.at[part])
    for part in numbers:
        alls[part].finish()
    grad_out[...] = full[...]
    for part in numbers:
        alls[part].drain()


def chunks_of(rows, size):
    return [(start, min(size, rows - start)) for start in range(0, rows, size)]


def adagrad_kernel(
    cuts, table, state, grad, phase, phase_state, rel_grad,
    new_table, new_state, new_phase, new_phase_state,
    table_now, grad_now, phase_now, rel_now, table_in, grad_in, out_sems,
):
    jobs = [
        (table, grad, table_now, grad_now, state, new_table, new_state, start, size)
        for start, size in cuts[0]
    ] + [
        (phase, rel_grad, phase_now, rel_now, phase_state, new_phase, new_phase_state, start, size)
        for start, size in cuts[1]
    ]

    def load(i):
        source, gradient, now, grad_at, _, _, _, start, size = jobs[i]
        cols = pl.ds(start, size)
        return (
            pltpu.make_async_copy(source.at[:, cols], now.at[:, cols], table_in.at[i]),
            pltpu.make_async_copy(gradient.at[:, cols], grad_at.at[:, cols], grad_in.at[i]),
        )

    def store(i):
        _, _, now, _, _, target, _, start, size = jobs[i]
        cols = pl.ds(start, size)
        return pltpu.make_async_copy(now.at[:, cols], target.at[:, cols], out_sems.at[i])

    for i in range(len(jobs)):
        for copy in load(i):
            copy.start()
    for i, (_, _, now, grad_at, old, _, new, start, size) in enumerate(jobs):
        for copy in load(i):
            copy.wait()
        cols = pl.ds(start, size)
        g = grad_at[: now.shape[0], cols].astype(F32)
        fresh = old[:, cols] + jnp.sum(g * g, 0, keepdims=True) * (1.0 / g.shape[0])
        new[:, cols] = fresh
        now[:, cols] = now[:, cols] - g * (RATE / jnp.sqrt(fresh))
        store(i).start()
    for i in range(len(jobs)):
        store(i).wait()


def adagrad(table, state, grad, phase, phase_state, rel_grad):
    width, rows = table.shape
    narrow, nrel = phase.shape
    cuts = (chunks_of(rows, 512), chunks_of(nrel, 1024))
    count = len(cuts[0]) + len(cuts[1])
    dma = pltpu.SemaphoreType.DMA
    new_table, new_state, new_phase, new_phase_state = pl.pallas_call(
        functools.partial(adagrad_kernel, cuts),
        out_shape=(
            jax.ShapeDtypeStruct((width, rows), F32),
            jax.ShapeDtypeStruct((1, rows), F32),
            jax.ShapeDtypeStruct((narrow, nrel), F32),
            jax.ShapeDtypeStruct((1, nrel), F32),
        ),
        in_specs=[HBM, VM, HBM, HBM, VM, HBM],
        out_specs=(HBM, VM, HBM, VM),
        scratch_shapes=[
            pltpu.VMEM((width, rows), F32),
            pltpu.VMEM((width, rows), BF16),
            pltpu.VMEM((narrow, nrel), F32),
            pltpu.VMEM(rel_grad.shape, BF16),
            dma((count,)), dma((count,)), dma((count,)),
        ],
        compiler_params=pltpu.CompilerParams(vmem_limit_bytes=VMEM_LIMIT),
        name="adagrad",
    )(table, state[None], grad, phase, phase_state[None], rel_grad)
    return new_table.T, new_state.reshape(rows), new_phase.T, new_phase_state.reshape(nrel)


VM = pl.BlockSpec(memory_space=pltpu.VMEM)
HBM = pl.BlockSpec(memory_space=pl.ANY)


def on_device(
    entity_table, entity_state, phase_table, phase_state,
    pull_rows, head_slot, tail_slot, neg_slot, relation,
):
    owners, dps = lax.axis_size("owner"), lax.axis_size("dp")
    table, phase = entity_table.T, phase_table.T
    width, rows = table.shape
    narrow, nrel = phase.shape
    triples = head_slot.shape[1]
    neg = neg_slot.shape[2]
    slots = jnp.concatenate([head_slot, tail_slot, neg_slot.reshape(1, -1)], 1)
    uses = slots.shape[1]
    pulls = owners * LANES
    requests = pull_rows.reshape(owners, 1, LANES)
    dma = pltpu.SemaphoreType.DMA
    chips = owners // 2
    padded = -(-narrow // 16) * 16
    share_tiles = -(-(nrel // LANES) // 16) * 2
    piece = -(-(share_tiles * padded // 16) // chips)
    nx, ny = grid_of(owners)
    parts = len(cut_parts(width))
    biggest = max(split_part(*part)[0][1] for part in cut_parts(width))
    grad, rel_total = pl.pallas_call(
        functools.partial(step_kernel, owners, triples // 2, neg),
        out_shape=(
            jax.ShapeDtypeStruct((width, rows), BF16),
            jax.ShapeDtypeStruct((padded, 8 * share_tiles * LANES), BF16),
        ),
        in_specs=[HBM, HBM, VM, VM, VM],
        out_specs=(VM, VM),
        scratch_shapes=[
            pltpu.VMEM((width, rows), F32),
            pltpu.VMEM((narrow, nrel), F32),
            pltpu.VMEM((width, rows), BF16),
            pltpu.VMEM((owners, 1, LANES), jnp.int32),
            pltpu.VMEM((pulls, LANES), jnp.int32),
            pltpu.VMEM((owners, width, LANES), BF16),
            pltpu.VMEM((width, pulls), BF16),
            pltpu.VMEM((width, uses), BF16),
            pltpu.VMEM((width, uses), BF16),
            pltpu.VMEM((width, triples), F32),
            pltpu.VMEM((narrow, triples), F32),
            pltpu.VMEM((narrow, triples), F32),
            pltpu.VMEM((padded, triples), F32),
            pltpu.VMEM((width, pulls), BF16),
            pltpu.VMEM((width, rows), F32),
            pltpu.VMEM((width, rows), BF16),
            pltpu.VMEM((parts, 6, biggest, rows // 4), BF16),
            pltpu.VMEM((width, rows), BF16),
            pltpu.VMEM((2, 4, padded, triples), BF16),
            pltpu.VMEM((2, 4, 1, triples), jnp.int32),
            pltpu.VMEM((chips * piece, 16, LANES), BF16),
            pltpu.VMEM((chips, piece, 16, LANES), BF16),
            pltpu.VMEM((2, nx, ny, 4, piece, 16, LANES), BF16),
            dma((2,)),
            dma, dma, dma, dma((3,)), dma((parts,)), dma((parts,)),
            dma((parts, 6)), dma((parts, 6)), dma((parts, 6)), dma((parts, 6)),
            dma((3,)), dma((3,)), dma((3,)), dma((3,)), dma((6,)), dma((6,)),
            dma, dma, dma((3,)), dma((3,)),
            dma((2, 3)), dma((2, 3)), dma((2, 6)), dma((2, 6)),
        ],
        compiler_params=pltpu.CompilerParams(
            collective_id=0, has_side_effects=True, vmem_limit_bytes=VMEM_LIMIT
        ),
        name="step",
    )(table, phase, requests, slots, relation)
    return adagrad(table, entity_state, grad, phase, phase_state, rel_total)


def solution(mesh):
    placed = (
        P("owner", None),
        P("owner"),
        P(),
        P(),
        P(("owner", "dp"), None, None),
        P(("owner", "dp"), None),
        P(("owner", "dp"), None),
        P(("owner", "dp"), None, None),
        P(("owner", "dp"), None),
    )
    return jax.shard_map(
        on_device,
        mesh=mesh,
        in_specs=placed,
        out_specs=(P("owner", None), P("owner"), P(), P()),
        check_vma=False,
    )
```

time: 166 us -> 158 us (0.952)
  Pallas kernels: 161 us -> 151 us
    pallas_call x1, Pallas kernels: 147 us -> 141 us  [on_device(): pl.pallas_call(functools.partial(step_kernel, owners, triples // 2, neg),...]
    pallas_call x2 -> x1, Pallas kernels: 13.7 us -> 10.1 us  [adagrad(): pl.pallas_call(functools.partial(adagrad_kernel, cuts), out_shape=(jax.Sh...]
where the time goes in v4:
time: 158 us; the launch traced here: 157 us
  Pallas kernels  151 us (96%)
  other arithmetic  2.74 us (2%)
  local copies, waits for them, and re-layouts  2.09 us (1%)
    pallas_call x1, Pallas kernels, on_device(): pl.pallas_call(functools.partial(step_kernel, owners, triples // 2, neg),...  141 us
    pallas_call x1, Pallas kernels, adagrad(): pl.pallas_call(functools.partial(adagrad_kernel, cuts), out_shape=(jax.Sh...  10.1 us

profile of v4, /device:TPU:1, one launch (start us, length us, event | category | flops | bytes accessed | tf_op | source)
XLA Modules:
  0.0 156.5 jit_solution(12101122484870966438)
XLA Ops:
  0.6 0.7 copy.13
  1.3 1.3 pad_add_fusion.slots
  2.6 1.4 broadcast_in_dim.7.phase_state
  4.0 140.9 %step.1 = (bf16[400,2048]{1,0:T(8,128)(2,1)}, bf16[208,8192]{1,0:T(8,128)(2,1)}) custom-call(f32[400,2048]{1,0:T(8,128)} %bitcast.11, f32[200,7424]{1,0:T(8,128)} %bitcast.9, s32[32,1,128]{2,1,0:T(1,128)} %bitcast.14, s32[1,3072]{1,0:T(1,128)} %pad_add_fusion.slots, s32[1,512]{1,0:T(1,128)} %relation.1), custom_call_target="tpu_custom_call" | custom-call | tf_op jit(solution)/shard_map/step/pallas_call | solution.py:798
  145.0 10.1 %adagrad.1 = (f32[400,2048]{1,0:T(8,128)}, f32[1,2048]{1,0:T(1,128)}, f32[200,7424]{1,0:T(8,128)}, f32[1,7424]{1,0:T(1,128)}) custom-call(f32[400,2048]{1,0:T(8,128)} %bitcast.12, f32[1,2048]{1,0:T(1,128)} %bitcast.15, bf16[400,2048]{1,0:T(8,128)(2,1)} %get-tuple-element.10.grad, f32[200,7424]{1,0:T(8,128)} %bitcast.10, ...), custom_call_target="tpu_custom_call" | custom-call | tf_op jit(solution)/shard_map/adagrad/pallas_call | solution.py:749
  155.1 1.4 reduce

commit v5 on v4

--- a/solution.py
+++ b/solution.py
@@ -267,7 +267,7 @@
 
 def step_kernel(
     owners, group, neg,
-    table_hbm, phase_hbm, requests, slots, relation,
+    table_hbm, phase_hbm, requests, head_slot, tail_slot, neg_slot, relation,
     grad_out, rel_out,
     table, phase, table_half, asked, asked_column, sent, pulled, used, grads,
     theta, cosine, sine, phase_grads,
@@ -397,8 +397,10 @@
     cosine[...] = jnp.cos(angle)
     sine[...] = jnp.sin(angle)
 
-    place = positions(slots[...], me, nx, ny)
-    uses = slots.shape[1]
+    slots = [head_slot[...], tail_slot[...]]
+    slots += [neg_slot[0, b : b + 1] for b in range(neg_slot.shape[1])]
+    place = positions(jnp.concatenate(slots, 1), me, nx, ny)
+    uses = place.shape[1]
     tile = 256
     for cut in range(3):
         low, high = cuts[cut], cuts[cut + 1]
@@ -645,14 +647,14 @@
             ring.finish()
         to_sibling(rel_sum, 2).start()
 
-    scatter(0, [(6, functools.partial(send_later, 2)), (7, sum_plane)])
+    scatter(0, [(6, functools.partial(send_later, 2))])
     sums[0].begin()
-    start_lines()
-    scatter(1, [(2, sums[0].relay), (4, start_sheets)])
+    sum_plane()
+    scatter(1, [(0, start_lines), (2, sums[0].relay)])
     sums[1].begin()
     scatter(2, [
-        (0, functools.partial(settle, 0)), (1, relay_sheets), (4, sums[1].relay),
-        (5, alls[0].relay), (7, start_core),
+        (0, functools.partial(settle, 0)), (1, start_sheets), (4, sums[1].relay),
+        (5, alls[0].relay), (7, relay_sheets),
     ])
     sums[2].begin()
     last = 2
@@ -666,12 +668,13 @@
 
     settle(1)
     sums[last].relay()
-    loop(0, 4, lambda z: lay(core, z))
     alls[1].relay()
     settle(last)
+    start_core()
+    alls[last].relay()
+    loop(0, 4, lambda z: lay(core, z))
     arrive(rel_sum.at[1 - core], core_recv.at[2])
     loop(0, 4, lambda z: lay(1 - core, z))
-    alls[last].relay()
 
     indices.drain()
     raw_ring.drain()
@@ -732,8 +735,8 @@
             copy.wait()
         cols = pl.ds(start, size)
         g = grad_at[: now.shape[0], cols].astype(F32)
-        fresh = old[:, cols] + jnp.sum(g * g, 0, keepdims=True) * (1.0 / g.shape[0])
-        new[:, cols] = fresh
+        fresh = old[cols].reshape(1, size) + jnp.sum(g * g, 0, keepdims=True) * (1.0 / g.shape[0])
+        new[cols] = fresh.reshape(size)
         now[:, cols] = now[:, cols] - g * (RATE / jnp.sqrt(fresh))
         store(i).start()
     for i in range(len(jobs)):
@@ -750,9 +753,9 @@
         functools.partial(adagrad_kernel, cuts),
         out_shape=(
             jax.ShapeDtypeStruct((width, rows), F32),
-            jax.ShapeDtypeStruct((1, rows), F32),
+            jax.ShapeDtypeStruct((rows,), F32),
             jax.ShapeDtypeStruct((narrow, nrel), F32),
-            jax.ShapeDtypeStruct((1, nrel), F32),
+            jax.ShapeDtypeStruct((nrel,), F32),
         ),
         in_specs=[HBM, VM, HBM, HBM, VM, HBM],
         out_specs=(HBM, VM, HBM, VM),
@@ -765,8 +768,8 @@
         ],
         compiler_params=pltpu.CompilerParams(vmem_limit_bytes=VMEM_LIMIT),
         name="adagrad",
-    )(table, state[None], grad, phase, phase_state[None], rel_grad)
-    return new_table.T, new_state.reshape(rows), new_phase.T, new_phase_state.reshape(nrel)
+    )(table, state, grad, phase, phase_state, rel_grad)
+    return new_table.T, new_state, new_phase.T, new_phase_state
 
 
 VM = pl.BlockSpec(memory_space=pltpu.VMEM)
@@ -783,8 +786,7 @@
     narrow, nrel = phase.shape
     triples = head_slot.shape[1]
     neg = neg_slot.shape[2]
-    slots = jnp.concatenate([head_slot, tail_slot, neg_slot.reshape(1, -1)], 1)
-    uses = slots.shape[1]
+    uses = 2 * triples + neg_slot.shape[1] * neg
     pulls = owners * LANES
     requests = pull_rows.reshape(owners, 1, LANES)
     dma = pltpu.SemaphoreType.DMA
@@ -801,7 +803,7 @@
             jax.ShapeDtypeStruct((width, rows), BF16),
             jax.ShapeDtypeStruct((padded, 8 * share_tiles * LANES), BF16),
         ),
-        in_specs=[HBM, HBM, VM, VM, VM],
+        in_specs=[HBM, HBM, VM, VM, VM, VM, VM],
         out_specs=(VM, VM),
         scratch_shapes=[
             pltpu.VMEM((width, rows), F32),
@@ -838,7 +840,7 @@
             collective_id=0, has_side_effects=True, vmem_limit_bytes=VMEM_LIMIT
         ),
         name="step",
-    )(table, phase, requests, slots, relation)
+    )(table, phase, requests, head_slot, tail_slot, neg_slot, relation)
     return adagrad(table, entity_state, grad, phase, phase_state, rel_total)
 
 

time: 158 us -> 149 us (0.943)
  Pallas kernels: 151 us -> 147 us
  other arithmetic: 2.74 us -> 0 us
  local copies, waits for them, and re-layouts: 2.09 us -> 0 us
    pallas_call x1, Pallas kernels: 141 us -> 137 us  [on_device(): pl.pallas_call(functools.partial(step_kernel, owners, triples // 2, neg),...]
where the time goes in v5:
time: 149 us; the launch traced here: 148 us
  Pallas kernels  147 us (99%)
    pallas_call x1, Pallas kernels, on_device(): pl.pallas_call(functools.partial(step_kernel, owners, triples // 2, neg),...  137 us
    pallas_call x1, Pallas kernels, adagrad(): pl.pallas_call(functools.partial(adagrad_kernel, cuts), out_shape=(jax.Sh...  10.1 us

profile of v5, /device:TPU:1, one launch (start us, length us, event | category | flops | bytes accessed | tf_op | source)
XLA Modules:
  0.0 147.8 jit_solution(5575175438720657456)
XLA Ops:
  0.6 136.9 %step.1 = (bf16[400,2048]{1,0:T(8,128)(2,1)}, bf16[208,8192]{1,0:T(8,128)(2,1)}) custom-call(f32[400,2048]{1,0:T(8,128)} %bitcast.7, f32[200,7424]{1,0:T(8,128)} %bitcast.5, s32[32,1,128]{2,1,0:T(1,128)} %bitcast.9, s32[1,512]{1,0:T(1,128)} %head_slot.1, s32[1,512]{1,0:T(1,128)} %tail_slot.1, s32[1,2,1024]{2,1,0:T(2,128)} %neg_slot.1, s32[1,512]{1,0:T(1,128)} %relation.1), custom_call_target="tpu_custom_call" | custom-call | tf_op jit(solution)/shard_map/step/pallas_call | solution.py:800
  137.5 10.1 %adagrad.1 = (f32[400,2048]{1,0:T(8,128)}, f32[2048]{0:T(1024)}, f32[200,7424]{1,0:T(8,128)}, f32[7424]{0:T(1024)}) custom-call(f32[400,2048]{1,0:T(8,128)} %bitcast.8, f32[2048]{0:T(1024)} %state.1, bf16[400,2048]{1,0:T(8,128)(2,1)} %get-tuple-element.10.grad, f32[200,7424]{1,0:T(8,128)} %bitcast.6, f32[7424]{0:T(1024)} %phase_state.1, ...), custom_call_target="tpu_custom_call" | custom-call | tf_op jit(solution)/shard_map/adagrad/pallas_call | solution.py:752

commit v6 on v5

--- a/solution.py
+++ b/solution.py
@@ -339,7 +339,7 @@
     load_table.wait()
     table_half[...] = table[...].astype(BF16)
 
-    cuts = (0, chips // 2, chips - chips // 4, chips)
+    cuts = (0, chips // 2, chips - chips // 4, chips - chips // 8, chips)
 
     def row_copy(cut, j, q, to):
         pltpu.make_async_remote_copy(
@@ -368,7 +368,7 @@
 
     arrive(asked, ask_recv)
     fetch(0, 0)
-    for cut in range(3):
+    for cut in range(4):
         loop(max(1, cuts[cut]), cuts[cut + 1], functools.partial(fetch, cut))
 
     load_phase.wait()
@@ -402,7 +402,7 @@
     place = positions(jnp.concatenate(slots, 1), me, nx, ny)
     uses = place.shape[1]
     tile = 256
-    for cut in range(3):
+    for cut in range(4):
         low, high = cuts[cut], cuts[cut + 1]
         if low == high:
             continue
@@ -830,7 +830,7 @@
             pltpu.VMEM((chips, piece, 16, LANES), BF16),
             pltpu.VMEM((2, nx, ny, 4, piece, 16, LANES), BF16),
             dma((2,)),
-            dma, dma, dma, dma((3,)), dma((parts,)), dma((parts,)),
+            dma, dma, dma, dma((4,)), dma((parts,)), dma((parts,)),
             dma((parts, 6)), dma((parts, 6)), dma((parts, 6)), dma((parts, 6)),
             dma((3,)), dma((3,)), dma((3,)), dma((3,)), dma((6,)), dma((6,)),
             dma, dma, dma((3,)), dma((3,)),

time: 149 us -> 148 us (level)
  Pallas kernels: 147 us -> 145 us
    pallas_call x1, Pallas kernels: 137 us -> 135 us  [on_device(): pl.pallas_call(functools.partial(step_kernel, owners, triples // 2, neg),...]
where the time goes in v6:
time: 148 us; the launch traced here: 146 us
  Pallas kernels  145 us (98%)
    pallas_call x1, Pallas kernels, on_device(): pl.pallas_call(functools.partial(step_kernel, owners, triples // 2, neg),...  135 us
    pallas_call x1, Pallas kernels, adagrad(): pl.pallas_call(functools.partial(adagrad_kernel, cuts), out_shape=(jax.Sh...  10.1 us

profile of v6, /device:TPU:1, one launch (start us, length us, event | category | flops | bytes accessed | tf_op | source)
XLA Modules:
  0.0 146.2 jit_solution(18015956976846982428)
XLA Ops:
  0.6 135.2 %step.1 = (bf16[400,2048]{1,0:T(8,128)(2,1)}, bf16[208,8192]{1,0:T(8,128)(2,1)}) custom-call(f32[400,2048]{1,0:T(8,128)} %bitcast.7, f32[200,7424]{1,0:T(8,128)} %bitcast.5, s32[32,1,128]{2,1,0:T(1,128)} %bitcast.9, s32[1,512]{1,0:T(1,128)} %head_slot.1, s32[1,512]{1,0:T(1,128)} %tail_slot.1, s32[1,2,1024]{2,1,0:T(2,128)} %neg_slot.1, s32[1,512]{1,0:T(1,128)} %relation.1), custom_call_target="tpu_custom_call" | custom-call | tf_op jit(solution)/shard_map/step/pallas_call | solution.py:800
  135.8 10.1 %adagrad.1 = (f32[400,2048]{1,0:T(8,128)}, f32[2048]{0:T(1024)}, f32[200,7424]{1,0:T(8,128)}, f32[7424]{0:T(1024)}) custom-call(f32[400,2048]{1,0:T(8,128)} %bitcast.8, f32[2048]{0:T(1024)} %state.1, bf16[400,2048]{1,0:T(8,128)(2,1)} %get-tuple-element.10.grad, f32[200,7424]{1,0:T(8,128)} %bitcast.6, f32[7424]{0:T(1024)} %phase_state.1, ...), custom_call_target="tpu_custom_call" | custom-call | tf_op jit(solution)/shard_map/adagrad/pallas_call | solution.py:752
